TPU v7x, 512 devices: a whole 4x4x16 slice. The times are simulated.
512 devices in a mesh: rows: 64 (over z, y), cols: 8 (over x, core).
Axes of the slice: x: 4, y: 4, z: 16, core: 2. Of those that a mesh axis runs over, the one named last changes fastest.
Arguments:
- tile_blocks: bfloat16 [64, 64, 128, 128], P('rows', 'cols'), as said below
- tile_row: int32 [64, 64], P('rows', 'cols'), may hold values from 0 to 1, as said below
- tile_col: int32 [64, 64], P('rows', 'cols'), may hold values from 0 to 3, as said below
- tile_count: int32 [64, 8], P('rows', 'cols'), may hold values from 4 to 8, as said below
- column_costs: float32 [4096], P('cols'), may hold values from 0.5 to 2
- demand: int32 [16384, 256], P('rows'), may hold values from 0 to 7
- primal_start: float32 [4096, 256], P('cols'), may hold values from 0 to 0.5
- dual_start: float32 [16384, 256], P('rows'), may hold values from -6 to 6
Outputs:
- solution: float32 [4096, 256], P('cols')
- dual_values: float32 [16384, 256], P('rows')
- primal_residual: float32 [16384, 256], P('rows')
- primal_weight: float32 [256], replicated
Inputs may be any that keep to these rules, and one draw needn't show every extreme that they name: Within one device the slots name distinct (tile_row, tile_col) pairs, all 8 of them; the first max(2, 4) slots name every block-row and every block-column of the device. `tile_col`: paired with tile_row slot by slot. `tile_count`: some device uses all 8 slots in every draw; only slots below a device's count hold blocks of A. `tile_blocks`: slots at or above a device's count hold values that are not part of A.
All inputs are finite; a program needn't handle non-finite values.
Results may differ from a plain program's by a relative error of at most 0.0003.
Values sent between devices are 32-bit elements; how exact they have to be, the bound alone decides.
A program may use at most 64 MiB of HBM per device.

v0:
```python
import jax
import jax.numpy as jnp
from jax import lax
from jax.sharding import PartitionSpec as P

ROW_BLOCKS = 2
COL_BLOCKS = 4
TILE = 128
SCENARIOS = 256
SWEEPS = 2
ITERS = 4


HIGHEST = lax.Precision.HIGHEST
EPSILON = 1e-06


def slot_tables(tile_row, tile_col, tile_count):
    live_mask = (jnp.arange(tile_row.shape[0], dtype=jnp.int32) < tile_count).astype(jnp.float32)
    row_hot = (tile_row[:, None] == jnp.arange(ROW_BLOCKS, dtype=jnp.int32)[None, :]).astype(
        jnp.float32
    ) * live_mask[:, None]
    col_hot = (tile_col[:, None] == jnp.arange(COL_BLOCKS, dtype=jnp.int32)[None, :]).astype(
        jnp.float32
    ) * live_mask[:, None]
    return (row_hot, col_hot)


def scaled_tiles(blocks, row_hot, col_hot, row_scale, col_scale):
    magnitude = jnp.abs(blocks.astype(jnp.float32))
    row_pick = jnp.einsum("tr,rk->tk", row_hot, row_scale, precision=HIGHEST)
    col_pick = jnp.einsum("tc,ck->tk", col_hot, col_scale, precision=HIGHEST)
    return magnitude * row_pick[:, :, None] * col_pick[:, None, :]


def extremes(scaled, row_hot, col_hot):
    row_part = jnp.max(row_hot.T[:, :, None] * jnp.max(scaled, axis=2)[None], axis=1)
    col_part = jnp.max(col_hot.T[:, :, None] * jnp.max(scaled, axis=1)[None], axis=1)
    return (row_part, col_part)


def totals(scaled, row_hot, col_hot):
    row_part = jnp.einsum("tr,tk->rk", row_hot, jnp.sum(scaled, axis=2), precision=HIGHEST)
    col_part = jnp.einsum("tc,tk->ck", col_hot, jnp.sum(scaled, axis=1), precision=HIGHEST)
    return (row_part, col_part)


def forward(blocks, row_hot, col_hot, vectors):
    picked = jnp.einsum("tc,cks->tks", col_hot, vectors, precision=HIGHEST)
    product = jnp.einsum("tij,tjs->tis", blocks.astype(jnp.float32), picked, precision=HIGHEST)
    return jnp.einsum("tr,tis->ris", row_hot, product, precision=HIGHEST)


def backward(blocks, row_hot, col_hot, vectors):
    picked = jnp.einsum("tr,rks->tks", row_hot, vectors, precision=HIGHEST)
    product = jnp.einsum("tij,tis->tjs", blocks.astype(jnp.float32), picked, precision=HIGHEST)
    return jnp.einsum("tc,tjs->cjs", col_hot, product, precision=HIGHEST)


def body(
    tile_blocks, tile_row, tile_col, tile_count, column_costs, demand, primal_start, dual_start
):
    blocks = tile_blocks[0]
    row_hot, col_hot = slot_tables(tile_row[0], tile_col[0], tile_count[0, 0])
    row_scale = jnp.ones((ROW_BLOCKS, TILE), jnp.float32)
    col_scale = jnp.ones((COL_BLOCKS, TILE), jnp.float32)
    for sweep_index in range(SWEEPS):
        scaled = scaled_tiles(blocks, row_hot, col_hot, row_scale, col_scale)
        row_part, col_part = extremes(scaled, row_hot, col_hot)
        row_max = lax.pmax(row_part, "cols")
        col_max = lax.pmax(col_part, "rows")
        row_scale = row_scale / jnp.sqrt(row_max + EPSILON)
        col_scale = col_scale / jnp.sqrt(col_max + EPSILON)
    scaled = scaled_tiles(blocks, row_hot, col_hot, row_scale, col_scale)
    row_part, col_part = totals(scaled, row_hot, col_hot)
    row_sum = lax.psum(row_part, "cols")
    col_sum = lax.psum(col_part, "rows")
    largest_row = lax.pmax(jnp.max(row_sum), "rows")
    largest_col = lax.pmax(jnp.max(col_sum), "cols")
    step_size = 0.95 / jnp.sqrt(largest_row * largest_col)
    cost_hat = col_scale * column_costs.reshape(COL_BLOCKS, TILE)
    demand_hat = row_scale[..., None] * demand.astype(jnp.float32).reshape(
        ROW_BLOCKS, TILE, SCENARIOS
    )
    primal = primal_start.reshape(COL_BLOCKS, TILE, SCENARIOS) / col_scale[..., None]
    dual_now = dual_start.reshape(ROW_BLOCKS, TILE, SCENARIOS) / row_scale[..., None]
    weight = jnp.ones((SCENARIOS,), jnp.float32)
    residual = demand_hat
    for iteration in range(ITERS):
        partial_costs = backward(blocks, row_hot, col_hot, row_scale[..., None] * dual_now)
        summed = lax.psum(partial_costs, "rows")
        gradient = cost_hat[..., None] - col_scale[..., None] * summed
        new_primal = jnp.maximum(primal - step_size / weight * gradient, 0.0)
        primal_moves = lax.psum(jnp.sum(jnp.square(new_primal - primal), axis=(0, 1)), "cols")
        extended = 2.0 * new_primal - primal
        demand_part = forward(blocks, row_hot, col_hot, col_scale[..., None] * extended)
        row_image = lax.psum(demand_part, "cols")
        residual = demand_hat - row_scale[..., None] * row_image
        new_dual = dual_now + step_size * weight * residual
        dual_moves = lax.psum(jnp.sum(jnp.square(new_dual - dual_now), axis=(0, 1)), "rows")
        weight = jnp.sqrt(weight * jnp.sqrt((dual_moves + EPSILON) / (primal_moves + EPSILON)))
        primal = new_primal
        dual_now = new_dual
    solution = (col_scale[..., None] * primal).reshape(COL_BLOCKS * TILE, SCENARIOS)
    dual_values = (row_scale[..., None] * dual_now).reshape(ROW_BLOCKS * TILE, SCENARIOS)
    return (solution, dual_values, residual.reshape(ROW_BLOCKS * TILE, SCENARIOS), weight)


def solution(mesh):
    return jax.shard_map(
        body,
        mesh=mesh,
        in_specs=(
            P("rows", "cols", None, None),
            P("rows", "cols"),
            P("rows", "cols"),
            P("rows", "cols"),
            P("cols"),
            P("rows", None),
            P("cols", None),
            P("rows", None),
        ),
        out_specs=(P("cols", None), P("rows", None), P("rows", None), P()),
        check_vma=False,
    )
```

profile of v0, /device:TPU:1, one launch (start us, length us, event | category | flops | bytes accessed | tf_op | source)
XLA Modules:
  0.0 1887.5 jit_solution(17377723446753162937)
XLA Ops:
  12.5 18.6 pmax.43
  31.2 117.1 %pmax.42 = f32[4,128]{1,0:T(4,128)S(1)} all-reduce(f32[4,128]{1,0:T(4,128)S(1)} %multiply_reduce_fusion.9), channel_id=1, replica_groups=mesh['rows'=64,'cols'=8] {'rows'}, use_global_device_ids=true, to_apply=%region_2.0 | all-reduce | flops 512 | bytes 4096 | tf_op jit(solution)/shard_map/pmax | solution.py:71
  149.2 42.0 %pmax.45 = f32[2,128]{1,0:T(2,128)S(1)} all-reduce(f32[2,128]{1,0:T(2,128)S(1)} %multiply_reduce_fusion.10), channel_id=1, replica_groups=mesh['rows'=64,'cols'=8] {'cols'}, use_global_device_ids=true, to_apply=%region_11.0 | all-reduce | flops 256 | bytes 2048 | tf_op jit(solution)/shard_map/pmax | solution.py:70
  194.3 1.8 fusion.66
  196.4 110.3 %pmax.44 = f32[4,128]{1,0:T(4,128)S(1)} all-reduce(f32[4,128]{1,0:T(4,128)S(1)} %multiply_reduce_fusion.8), channel_id=1, replica_groups=mesh['rows'=64,'cols'=8] {'rows'}, use_global_device_ids=true, to_apply=%region_8.0 | all-reduce | flops 512 | bytes 4096 | tf_op jit(solution)/shard_map/pmax | solution.py:71
  307.5 40.1 %psum.126 = f32[2,128]{1,0:T(2,128)S(1)} all-reduce(f32[2,128]{1,0:T(2,128)S(1)} %fusion.118), channel_id=1, replica_groups=mesh['rows'=64,'cols'=8] {'cols'}, use_global_device_ids=true, to_apply=%region_13.0 | all-reduce | flops 256 | bytes 2048 | tf_op jit(solution)/shard_map/psum | solution.py:76
  348.3 112.7 %psum.127 = f32[4,128]{1,0:T(4,128)S(1)} all-reduce(f32[4,128]{1,0:T(4,128)S(1)} %fusion.55), channel_id=1, replica_groups=mesh['rows'=64,'cols'=8] {'rows'}, use_global_device_ids=true, to_apply=%region_17.0 | all-reduce | flops 512 | bytes 4096 | tf_op jit(solution)/shard_map/psum | solution.py:77
  461.6 111.3 %pmax.46 = f32[]{:T(128)} all-reduce(f32[]{:T(128)} %reduce_max.98), channel_id=1, replica_groups=mesh['rows'=64,'cols'=8] {'rows'}, use_global_device_ids=true, to_apply=%region_15.0 | all-reduce | flops 1 | bytes 8 | tf_op jit(solution)/shard_map/pmax | solution.py:78
  572.9 68.0 %pmax.47 = f32[]{:T(128)} all-reduce(f32[]{:T(128)} %reduce_max.99), channel_id=1, replica_groups=mesh['rows'=64,'cols'=8] {'cols'}, use_global_device_ids=true, to_apply=%region_19.0 | all-reduce | flops 1 | bytes 8 | tf_op jit(solution)/shard_map/pmax | solution.py:79
  642.6 2.2 multiply_reduce_fusion.3
  650.2 64.3 %all-reduce.11.cloned.1.call-done = f32[2,128,256]{2,1,0:T(8,128)} async-done(((f32[2,128,256]{2,1,0:T(8,128)}), f32[2,128,256]{2,1,0:T(8,128)}) %all-reduce.11.cloned.1.call-update) | async-done | bytes 262160 | tf_op jit(solution)/shard_map/psum | solution.py:97
  714.5 1.7 multiply_reduce_fusion.7
  719.8 1.8 fusion.65
  722.3 13.8 psum.131
  736.8 116.2 %psum.130 = f32[256]{0:T(256)S(1)} all-reduce(f32[256]{0:T(256)S(1)} %copy-done.21), channel_id=1, replica_groups=mesh['rows'=64,'cols'=8] {'rows'}, use_global_device_ids=true, to_apply=%region_23.0 | all-reduce | flops 256 | bytes 2048 | tf_op jit(solution)/shard_map/psum | solution.py:100
  853.1 125.2 %all-reduce.13.cloned.1.call-done = f32[4,128,256]{2,0,1:T(4,128)} async-done(((f32[4,128,256]{2,0,1:T(4,128)}), f32[4,128,256]{2,0,1:T(4,128)}) %all-reduce.13.cloned.1.call-update) | async-done | bytes 524304 | tf_op jit(solution)/shard_map/psum | solution.py:91
  983.6 2.2 fusion.74
  986.8 78.0 %all-reduce.15.cloned.1.call-done = f32[2,128,256]{2,1,0:T(8,128)} async-done(((f32[2,128,256]{2,1,0:T(8,128)}), f32[2,128,256]{2,1,0:T(8,128)}) %all-reduce.15.cloned.1.call-update) | async-done | bytes 262160 | tf_op jit(solution)/shard_map/psum | solution.py:97
  1069.9 3.0 fusion.64
  1073.0 13.9 psum.135
  1086.8 116.3 %psum.134 = f32[256]{0:T(256)S(1)} all-reduce(f32[256]{0:T(256)S(1)} %get-tuple-element.20), channel_id=1, replica_groups=mesh['rows'=64,'cols'=8] {'rows'}, use_global_device_ids=true, to_apply=%region_29.0 | all-reduce | flops 256 | bytes 2048 | tf_op jit(solution)/shard_map/psum | solution.py:100
  1204.3 125.3 %all-reduce.17.cloned.1.call-done = f32[4,128,256]{2,0,1:T(4,128)} async-done(((f32[4,128,256]{2,0,1:T(4,128)}), f32[4,128,256]{2,0,1:T(4,128)}) %all-reduce.17.cloned.1.call-update) | async-done | bytes 524304 | tf_op jit(solution)/shard_map/psum | solution.py:91
  1329.6 2.0 multiply_reduce_fusion.1
  1336.6 78.0 %all-reduce.19.cloned.1.call-done = f32[2,128,256]{2,1,0:T(8,128)} async-done(((f32[2,128,256]{2,1,0:T(8,128)}), f32[2,128,256]{2,1,0:T(8,128)}) %all-reduce.19.cloned.1.call-update) | async-done | bytes 262160 | tf_op jit(solution)/shard_map/psum | solution.py:97
  1419.3 1.8 fusion.63
  1421.8 13.8 psum.139
  1436.3 116.3 %psum.138 = f32[256]{0:T(256)S(1)} all-reduce(f32[256]{0:T(256)S(1)} %copy-done.15), channel_id=1, replica_groups=mesh['rows'=64,'cols'=8] {'rows'}, use_global_device_ids=true, to_apply=%region_35.0 | all-reduce | flops 256 | bytes 2048 | tf_op jit(solution)/shard_map/psum | solution.py:100
  1553.7 124.1 %all-reduce.21.cloned.1.call-done = f32[4,128,256]{2,0,1:T(4,128)} async-done(((f32[4,128,256]{2,0,1:T(4,128)}), f32[4,128,256]{2,0,1:T(4,128)}) %all-reduce.21.cloned.1.call-update) | async-done | bytes 524304 | tf_op jit(solution)/shard_map/psum | solution.py:91
  1677.8 2.5 fusion.8
  1685.7 22.5 %psum.143 = f32[256]{0:T(256)S(1)} all-reduce(f32[256]{0:T(256)S(1)} %get-tuple-element.32), channel_id=1, replica_groups=mesh['rows'=64,'cols'=8] {'cols'}, use_global_device_ids=true, to_apply=%region_43.0 | all-reduce | flops 256 | bytes 2048 | tf_op jit(solution)/shard_map/psum | solution.py:94
  1708.2 53.8 %all-reduce.23.cloned.1.call-done = f32[2,128,256]{2,1,0:T(8,128)} async-done(((f32[2,128,256]{2,1,0:T(8,128)}), f32[2,128,256]{2,1,0:T(8,128)}) %all-reduce.23.cloned.1.call-update) | async-done | bytes 262160 | tf_op jit(solution)/shard_map/psum | solution.py:97
  1763.9 116.0 %psum.142 = f32[256]{0:T(256)S(1)} all-reduce(f32[256]{0:T(256)S(1)} %get-tuple-element.10), channel_id=1, replica_groups=mesh['rows'=64,'cols'=8] {'rows'}, use_global_device_ids=true, to_apply=%region_41.0 | all-reduce | flops 256 | bytes 2048 | tf_op jit(solution)/shard_map/psum | solution.py:100
  (135 shorter events, 54.2 us)
Async XLA Ops:
  7.2 141.6 %copy-start = (bf16[1,8,128,128]{3,2,1,0:T(8,128)(2,1)S(1)}, bf16[1,8,128,128]{3,2,1,0:T(8,128)(2,1)}, u32[]{:S(2)}) copy-start(bf16[1,8,128,128]{3,2,1,0:T(8,128)(2,1)} %param.8) | copy-start | bytes 786436
  7.2 635.4 %all-reduce.9.cloned.1.call-start = ((), (), s32[]{:S(2)}) async-start(), calls=%async_computation | async-start | bytes 1048576 | tf_op jit(solution)/shard_map/psum | solution.py:91
  10.1 138.2 %copy-start.9 = (s32[1,8]{1,0:T(1,128)S(1)}, s32[1,8]{1,0:T(1,128)}, u32[]{:S(2)}) copy-start(s32[1,8]{1,0:T(1,128)} %param.10) | copy-start | bytes 100
  10.1 138.4 %copy-start.8 = (s32[1,8]{1,0:T(1,128)S(1)}, s32[1,8]{1,0:T(1,128)}, u32[]{:S(2)}) copy-start(s32[1,8]{1,0:T(1,128)} %param.9) | copy-start | bytes 100
  11.0 180.2 %copy-start.5 = (f32[256,256]{1,0:T(8,128)S(1)}, f32[256,256]{1,0:T(8,128)}, u32[]{:S(2)}) copy-start(f32[256,256]{1,0:T(8,128)} %param.15) | copy-start | bytes 786436
  196.1 446.5 %copy-start.6 = (f32[512,256]{1,0:T(8,128)S(1)}, f32[512,256]{1,0:T(8,128)}, u32[]{:S(2)}) copy-start(f32[512,256]{1,0:T(8,128)} %param.14) | copy-start | bytes 1572868
  196.1 518.4 %all-reduce.11.cloned.1.call-start = ((), (), s32[]{:S(2)}) async-start(), calls=%async_computation.1 | async-start | bytes 524288 | tf_op jit(solution)/shard_map/psum | solution.py:97
  196.4 110.3 %copy-start.22 = (f32[512]{0:T(512)S(1)}, f32[512]{0:T(512)}, u32[]{:S(2)}) copy-start(f32[512]{0:T(512)} %param.12) | copy-start | bytes 6148
  649.6 64.9 %copy-start.1 = (s32[256,256]{1,0:T(8,128)S(1)}, s32[256,256]{1,0:T(8,128)}, u32[]{:S(2)}) copy-start(s32[256,256]{1,0:T(8,128)} %param.13) | copy-start | bytes 786436
  649.7 328.6 %all-reduce.13.cloned.1.call-start = ((), (), s32[]{:S(2)}) async-start(), calls=%async_computation.2 | async-start | bytes 1048576 | tf_op jit(solution)/shard_map/psum | solution.py:91
  716.2 0.7 copy-start.2
  721.6 0.7 copy-start.18
  721.6 343.2 %all-reduce.15.cloned.1.call-start = ((), (), s32[]{:S(2)}) async-start(), calls=%async_computation.3 | async-start | bytes 524288 | tf_op jit(solution)/shard_map/psum | solution.py:97
  736.1 0.7 copy-start.21
  986.6 78.3 %copy-start.3 = (f32[2,128,256]{2,1,0:T(8,128)S(1)}, f32[2,128,256]{2,1,0:T(8,128)}, u32[]{:S(2)}) copy-start(f32[2,128,256]{2,1,0:T(8,128)} %copy-done.2) | copy-start | bytes 786436
  986.6 343.0 %all-reduce.17.cloned.1.call-start = ((), (), s32[]{:S(2)}) async-start(), calls=%async_computation.4 | async-start | bytes 1048576 | tf_op jit(solution)/shard_map/psum | solution.py:91
  1072.9 341.7 %all-reduce.19.cloned.1.call-start = ((), (), s32[]{:S(2)}) async-start(), calls=%async_computation.5 | async-start | bytes 524288 | tf_op jit(solution)/shard_map/psum | solution.py:97
  1203.7 0.6 copy-start.11
  1336.3 78.3 %copy-start.16 = (f32[256]{0:T(256)S(1)}, f32[256]{0:T(256)}, u32[]{:S(2)}) copy-start(f32[256]{0:T(256)} %get-tuple-element.18) | copy-start | bytes 3076
  1336.3 341.4 %all-reduce.21.cloned.1.call-start = ((), (), s32[]{:S(2)}) async-start(), calls=%async_computation.6 | async-start | bytes 1048576 | tf_op jit(solution)/shard_map/psum | solution.py:91
  1421.1 0.7 copy-start.17
  1421.1 340.8 %all-reduce.23.cloned.1.call-start = ((), (), s32[]{:S(2)}) async-start(), calls=%async_computation.7 | async-start | bytes 524288 | tf_op jit(solution)/shard_map/psum | solution.py:97
  1435.6 0.7 copy-start.15
  1436.3 116.3 %copy-start.12 = (f32[256]{0:T(256)S(1)}, f32[256]{0:T(256)}, u32[]{:S(2)}) copy-start(f32[256]{0:T(256)} %copy-done.11) | copy-start | bytes 3076
  1553.1 0.6 copy-start.13
  1553.7 124.1 %copy-start.19 = (f32[256]{0:T(256)}, f32[256]{0:T(256)S(1)}, u32[]{:S(2)}) copy-start(f32[256]{0:T(256)S(1)} %broadcast_divide_fusion.1) | copy-start | bytes 3076
  1682.9 1.1 copy-start.7
  1683.6 0.7 copy-start.20
  1708.2 53.8 %copy-start.10 = (f32[256]{0:T(256)S(1)}, f32[256]{0:T(256)}, u32[]{:S(2)}) copy-start(f32[256]{0:T(256)} %get-tuple-element.12) | copy-start | bytes 3076
  1763.0 0.8 copy-start.4
  1763.9 116.0 %copy-start.14 = (f32[256]{0:T(256)S(1)}, f32[256]{0:T(256)}, u32[]{:S(2)}) copy-start(f32[256]{0:T(256)} %copy-done.13) | copy-start | bytes 3076
Sparse Core Ops, SparseCore 0:
  196.2 245.9 all-reduce.8
  649.8 64.6 all-reduce.10
  721.7 256.5 all-reduce.12
  986.7 78.0 all-reduce.14
  1073.0 256.5 all-reduce.16
  1336.4 78.1 all-reduce.18
  1421.2 256.5 all-reduce.20
  1683.8 78.0 all-reduce.22
where the time goes:
time: 1920 us; the launch traced here: 1890 us
  blocking collectives  1150 us (60%)
  waiting for transfers between devices  649 us (34%)
  matrix products  37.3 us (2%)
  other arithmetic  19.7 us (1%)
    psum x4, blocking collectives, body(): lax.psum(jnp.sum(jnp.square(new_dual - dual_now), axis=(0, 1)), 'rows')  465 us
    psum x4, waiting for transfers between devices, body(): summed = lax.psum(partial_costs, 'rows')  375 us
    psum x4, waiting for transfers between devices, body(): row_image = lax.psum(demand_part, 'cols')  274 us
    pmax x2, blocking collectives, body(): col_max = lax.pmax(col_part, 'rows')  227 us
    psum x1, blocking collectives, body(): col_sum = lax.psum(col_part, 'rows')  113 us
    pmax x1, blocking collectives, body(): largest_row = lax.pmax(jnp.max(row_sum), 'rows')  111 us
    pmax x1, blocking collectives, body(): largest_col = lax.pmax(jnp.max(col_sum), 'cols')  68 us
    psum x4, blocking collectives, body(): lax.psum(jnp.sum(jnp.square(new_primal - primal), axis=(0, 1)), 'cols')  64 us
  transfers between devices with their start and end apart: 8, of which 7 were waited for; matrix products, arithmetic and copies ran while one was open for 0% of the time, Pallas kernels for 0%

commit v1 on v0

v1 whole, which is shorter than its diff:
```python
import functools

import jax
import jax.numpy as jnp
from jax import lax
from jax.experimental import pallas as pl
from jax.experimental.pallas import tpu as pltpu
from jax.sharding import PartitionSpec as P

NZ, NY, NX, NK = 16, 4, 4, 2
NS = NY * NK
SCEN = 32
HALVES = 2
W = SCEN // HALVES
SR = W // 2 + W // 16
ITERS = 4
EPSILON = 1e-06
MESH = pl.DeviceIdType.MESH
F32, BF16 = jnp.float32, jnp.bfloat16


def kernel(
    row_ref, col_ref, count_ref, tiles_ref, costs_ref, demand_ref, primal_ref, dual_ref,
    sol_ref, dv_ref, res_ref, w_ref,
    la, ab, at, dd, yd, pt, px, cost, rsc, rsr, csr, part, rx, cz, g, rsb, gs, mrow, fx, xs, ydo, solt, drt, mz, wy,
    dd_s, dd_r, la_s, la_r, sb_s, sb_r, pt_s, pt_r, ct_s, ct_r, rx_s, rx_r, cz_s, cz_r,
    rs_s, rs_r, ag_s, ag_r, fx_s, fx_r, so_s, so_r, dr_s, dr_r, mz_s, mz_r, wy_s, wy_r,
):
    rows, cols = lax.axis_index("rows"), lax.axis_index("cols")
    z, y, x, k = rows // NY, rows % NY, cols // NK, cols % NK
    s = y * NK + k

    def dev(zz, yy, xx, kk):
        return (zz * NY + yy, xx * NK + kk)

    def put(src, dst, ss, rs, device):
        pltpu.make_async_remote_copy(
            src_ref=src, dst_ref=dst, send_sem=ss, recv_sem=rs, device_id=device, device_id_type=MESH
        ).start()

    def drain(ref, sem):
        pltpu.make_async_copy(ref, ref, sem).wait()

    def z_far_first(send):
        def step(i, carry):
            turn = (i + 1) // 2
            d = 8 + turn - 2 * turn * (i % 2)
            send(d, (z + d) % NZ)
            return carry

        lax.fori_loop(0, NZ - 1, step, 0)

    def scen(block):
        return pl.ds(pl.multiple_of(SCEN * block, SCEN), SCEN)

    sibling = dev(z, y, x, 1 - k)
    y_others = [(y + d) % NY for d in (1, 3, 2)]
    x_others = [(x + d) % NX for d in (2, 1, 3)]
    s_others = [(s + d) % NS for d in (4, 3, 5, 2, 6, 1, 7)]

    barrier = pltpu.get_barrier_semaphore()

    def greet(d, zz):
        pl.semaphore_signal(barrier, inc=1, device_id=dev(zz, y, x, k), device_id_type=MESH)

    z_far_first(greet)
    for xx in x_others:
        pl.semaphore_signal(barrier, inc=1, device_id=dev(z, y, xx, k), device_id_type=MESH)
    for ss in s_others:
        pl.semaphore_signal(barrier, inc=1, device_id=dev(z, ss // NK, x, ss % NK), device_id_type=MESH)

    for rb in range(2):
        for cb in range(4):
            slot = jnp.int32(0)
            for t in range(8):
                same = jnp.logical_and(row_ref[0, t] == rb, col_ref[0, t] == cb)
                slot = jnp.where(same, t, slot)
            live = slot < count_ref[0, 0]
            block = tiles_ref[slot].astype(F32)
            la[s, 128 * rb : 128 * rb + 128, 128 * cb : 128 * cb + 128] = jnp.where(live, block, 0.0)
    for a in range(2):
        dd[0, a] = dual_ref[128 * a : 128 * a + 128, :].T
        dd[1, a] = demand_ref[128 * a : 128 * a + 128, :].astype(F32).T
    for c in range(4):
        pt[c] = primal_ref[128 * c : 128 * c + 128, :].T
    cost[k, 0:4, :] = costs_ref[...]
    cost[k, 4:8, :] = jnp.zeros((4, 128), F32)
    for a in range(2):
        for kind in range(2):
            yd[kind, 2 * y + a] = dd[kind, a, scen(s), :]
    for c in range(4):
        px[4 * k + c] = pt[c, scen(s), :]

    pl.semaphore_wait(barrier, NZ - 1 + NX - 1 + NS - 1)

    put(la.at[s], la.at[s], sb_s, sb_r.at[y], sibling)
    put(
        pt.at[:, scen(2 * y + 1 - k), :], px.at[pl.ds(4 * k, 4)], pt_s, pt_r, sibling
    )
    put(cost.at[k], cost.at[k], ct_s, ct_r, sibling)
    for yy in y_others:
        put(
            dd.at[:, :, scen(yy * NK + k), :], yd.at[:, pl.ds(2 * y, 2)], dd_s, dd_r, dev(z, yy, x, k)
        )
    for yy in y_others:
        put(la.at[s], la.at[s], la_s, la_r.at[y], dev(z, yy, x, k))
    for d in (3, 1, 2):
        yy = (y + d) % NY
        block = yy * NK + k
        drain(la.at[block], la_r.at[yy])
        put(la.at[block], la.at[block], sb_s, sb_r.at[yy], sibling)
    for yy in range(NY):
        drain(la.at[yy * NK + 1 - k], sb_r.at[yy])
    drain(px.at[pl.ds(0, 4)], pt_r)
    drain(cost.at[0], ct_r)
    drain(yd.at[:, pl.ds(0, 6)], dd_r)

    def partials(op, reduce, scaled):
        def step(i, accs):
            row_acc, new = None, []
            for j in range(8):
                tile = jnp.abs(
                    la[
                        2 * (i // 2) + j // 4,
                        pl.ds(pl.multiple_of(128 * (i % 2), 128), 128),
                        128 * (j % 4) : 128 * (j % 4) + 128,
                    ]
                )
                if scaled:
                    tile = tile * rsc[i] * csr[j : j + 1, :]
                row_acc = tile if row_acc is None else op(row_acc, tile)
                new.append(op(accs[j], reduce(tile.reshape(16, 8, 128), axis=0)))
            part[0, pl.ds(i, 1), :] = reduce(row_acc.T, axis=0, keepdims=True)
            return tuple(new)

        accs = lax.fori_loop(0, 8, step, tuple(jnp.zeros((8, 128), F32) for _ in range(8)))
        for j in range(8):
            part[1, j : j + 1, :] = reduce(accs[j], axis=0, keepdims=True)

    def send_x(use, value):
        rx[use, x] = value
        for xx in x_others:
            put(rx.at[use, x], rx.at[use, x], rx_s.at[use], rx_r.at[use], dev(z, y, xx, k))

    def send_z(use, value):
        cz[use, z] = value
        z_far_first(
            lambda d, zz: put(cz.at[use, z], cz.at[use, z], cz_s.at[use], cz_r.at[use], dev(zz, y, x, k))
        )

    def wait_x(use):
        drain(rx.at[use, pl.ds(0, NX - 1)], rx_r.at[use])
        drain(rx.at[use, pl.ds(0, NX - 1)], rx_s.at[use])

    def wait_z(use):
        drain(cz.at[use, pl.ds(0, NZ - 1)], cz_r.at[use])
        drain(cz.at[use, pl.ds(0, NZ - 1)], cz_s.at[use])

    def rescale(use):
        wait_x(use)
        rsr[...] = rsr[...] / jnp.sqrt(jnp.max(rx[use], axis=0) + EPSILON)
        for i in range(8):
            rsc[i] = jnp.broadcast_to(rsr[i : i + 1, :], (128, 128)).T
        wait_z(use)
        csr[...] = csr[...] / jnp.sqrt(jnp.max(cz[use], axis=0) + EPSILON)

    def product(value, matrix):
        high = value.astype(BF16)
        low = (value - high.astype(F32)).astype(BF16)
        both = jnp.dot(jnp.concatenate([high, low], axis=0), matrix[...], preferred_element_type=F32)
        return both[:W] + both[W:]

    def backward(h, duals, moves):
        result = product(jnp.concatenate(duals, axis=1), ab)
        for j in range(8):
            for q in range(2):
                g[h, 2 * j + q, 0 : W // 2, :] = result[
                    q * (W // 2) : (q + 1) * (W // 2), 128 * j : 128 * j + 128
                ]
        n = W // 16
        for i in range(16):
            g[h, i, W // 2 : SR, :] = moves[i * n : (i + 1) * n, :]
        z_far_first(
            lambda d, zz: put(g.at[h, zz], rsb.at[h, d - 1], rs_s.at[h], rs_r.at[h], dev(zz, y, x, k))
        )

    def sum_and_spread(h):
        drain(rsb.at[h], rs_r.at[h])
        total = g[h, z]
        for d in range(NZ - 1):
            total = total + rsb[h, d]
        gs[h, z] = total
        z_far_first(
            lambda d, zz: put(gs.at[h, z], gs.at[h, z], ag_s.at[h], ag_r.at[h], dev(zz, y, x, k))
        )
        drain(rsb.at[h], rs_s.at[h])

    def part_of(h):
        return slice(h * W, (h + 1) * W)

    rsr[...] = jnp.ones((8, 128), F32)
    csr[...] = jnp.ones((8, 128), F32)
    partials(jnp.maximum, jnp.max, False)
    send_x(0, part[0])
    send_z(0, part[1])
    for b in range(8):
        ab[256 * (b // 2) : 256 * (b // 2) + 256, 512 * (b % 2) : 512 * (b % 2) + 512] = la[b].astype(BF16)
    for h in range(HALVES):
        backward(h, [yd[0, i, part_of(h), :] for i in range(8)], jnp.zeros((W, 128), F32))
    rescale(0)
    partials(jnp.maximum, jnp.max, True)
    send_x(1, part[0])
    send_z(1, part[1])
    for h in range(HALVES):
        sum_and_spread(h)
    for b in range(8):
        at[512 * (b % 2) : 512 * (b % 2) + 512, 256 * (b // 2) : 256 * (b // 2) + 256] = la[b].T.astype(BF16)
    rescale(1)
    partials(jnp.add, jnp.sum, True)
    send_x(2, part[0])
    send_z(2, part[1])
    for i in range(8):
        yd[0, i] = yd[0, i] / rsr[i : i + 1, :]
        yd[1, i] = yd[1, i] * rsr[i : i + 1, :]
        px[i] = px[i] / csr[i : i + 1, :]
    part[1] = csr[...] * jnp.concatenate([cost[0, 0:4, :], cost[1, 0:4, :]], axis=0)
    wait_x(2)
    row_sum = rx[2, 0] + rx[2, 1] + rx[2, 2] + rx[2, 3]
    send_z(3, row_sum)
    wait_z(2)
    col_sum = cz[2, 0]
    for i in range(1, NZ):
        col_sum = col_sum + cz[2, i]
    send_x(3, col_sum)
    wait_x(3)
    wait_z(3)

    def largest(tiles):
        return jnp.max(jnp.max(jnp.max(tiles, axis=0), axis=1, keepdims=True), axis=0, keepdims=True)

    step_size = 0.95 / jnp.sqrt(largest(cz[3]) * largest(rx[3]))

    weight = [jnp.ones((W, 1), F32) for _ in range(HALVES)]
    primal_moves = [None] * HALVES
    dual_moves = [None] * HALVES
    for t in range(ITERS):
        slot = t % 2
        last = t == ITERS - 1
        if t > 0:
            for h in range(HALVES):
                sum_and_spread(h)
        for h in range(HALVES):
            drain(gs.at[h, pl.ds(0, NZ - 1)], ag_r.at[h])
            if t > 0:
                n = W // 16
                for i in range(16):
                    mrow[h, i * n : (i + 1) * n, :] = gs[h, i, W // 2 : SR, :]
                moved = jnp.sum(mrow[h], axis=1, keepdims=True)
                weight[h] = jnp.sqrt(
                    weight[h] * jnp.sqrt((moved + EPSILON) / (primal_moves[h] + EPSILON))
                )
            rate = step_size / weight[h]
            moves, extended = jnp.zeros((W, 128), F32), []
            for j in range(8):
                scale = csr[j : j + 1, :]
                summed = jnp.concatenate(
                    [gs[h, 2 * j, 0 : W // 2, :], gs[h, 2 * j + 1, 0 : W // 2, :]], axis=0
                )
                old = px[j, part_of(h), :]
                new = jnp.maximum(old - rate * (part[1, j : j + 1, :] - scale * summed), 0.0)
                moves = moves + jnp.square(new - old)
                extended.append(scale * (2.0 * new - old))
                px[j, part_of(h), :] = new
                if last:
                    xs[j, part_of(h), :] = scale * new
            image = product(jnp.concatenate(extended, axis=1), at)
            for i in range(8):
                fx[slot, h, x, i] = image[:, 128 * i : 128 * i + 128]
            fx[slot, h, x, 8] = moves
            for xx in x_others:
                put(
                    fx.at[slot, h, x], fx.at[slot, h, x], fx_s.at[slot, h], fx_r.at[slot, h], dev(z, y, xx, k)
                )
            drain(gs.at[h, pl.ds(0, NZ - 1)], ag_s.at[h])
        if last:
            for c in range(4):
                solt[c, scen(s), :] = xs[4 * k + c]
            for ss in s_others:
                put(
                    xs.at[pl.ds(4 * (ss % NK), 4)], solt.at[:, scen(s), :], so_s, so_r,
                    dev(z, ss // NK, x, ss % NK),
                )
        for h in range(HALVES):
            drain(fx.at[slot, h, pl.ds(0, NX - 1)], fx_r.at[slot, h])
            rate = step_size * weight[h]
            moves, duals = jnp.zeros((W, 128), F32), []
            for i in range(8):
                scale = rsr[i : i + 1, :]
                image = fx[slot, h, 0, i] + fx[slot, h, 1, i] + fx[slot, h, 2, i] + fx[slot, h, 3, i]
                residual = yd[1, i, part_of(h), :] - scale * image
                old = yd[0, i, part_of(h), :]
                new = old + rate * residual
                moves = moves + jnp.square(new - old)
                yd[0, i, part_of(h), :] = new
                duals.append(scale * new)
                if last:
                    ydo[0, i, part_of(h), :] = scale * new
                    ydo[1, i, part_of(h), :] = residual
            primal_moves[h] = jnp.sum(
                fx[slot, h, 0, 8] + fx[slot, h, 1, 8] + fx[slot, h, 2, 8] + fx[slot, h, 3, 8],
                axis=1, keepdims=True,
            )
            if last:
                dual_moves[h] = jnp.sum(moves, axis=1, keepdims=True)
            else:
                backward(h, duals, moves)
            drain(fx.at[slot, h, pl.ds(0, NX - 1)], fx_s.at[slot, h])

    lane = lax.broadcasted_iota(jnp.int32, (8, 128), 1)

    def packed(columns):
        column = jnp.concatenate(columns, axis=0)
        tile = jnp.zeros((8, 128), F32)
        for q in range(4):
            tile = jnp.where(lane == q, column[8 * q : 8 * q + 8], tile)
        return tile

    mz[z] = packed(dual_moves)
    z_far_first(lambda d, zz: put(mz.at[z], mz.at[z], mz_s, mz_r, dev(zz, y, x, k)))
    for a in range(2):
        for kind in range(2):
            drt[kind, a, scen(s), :] = ydo[kind, 2 * y + a]
    for ss in s_others:
        put(
            ydo.at[:, pl.ds(2 * (ss // NK), 2)], drt.at[:, :, scen(s), :], dr_s, dr_r,
            dev(z, ss // NK, x, ss % NK),
        )
    drain(solt.at[:, pl.ds(0, SCEN * (NS - 1)), :], so_r)
    for c in range(4):
        sol_ref[128 * c : 128 * c + 128, :] = solt[c].T
    drain(mz.at[pl.ds(0, NZ - 1)], mz_r)
    moved = mz[0]
    for i in range(1, NZ):
        moved = moved + mz[i]
    wy[s] = jnp.sqrt(
        packed(weight) * jnp.sqrt((moved + EPSILON) / (packed(primal_moves) + EPSILON))
    )
    for ss in s_others:
        put(wy.at[s], wy.at[s], wy_s, wy_r, dev(z, ss // NK, x, ss % NK))
    drain(drt.at[:, :, pl.ds(0, SCEN * (NS - 1)), :], dr_r)
    for a in range(2):
        dv_ref[128 * a : 128 * a + 128, :] = drt[0, a].T
        res_ref[128 * a : 128 * a + 128, :] = drt[1, a].T
    drain(wy.at[pl.ds(0, NS - 1)], wy_r)
    gathered = jnp.zeros((8, 128), F32)
    for b in range(NS):
        tile = jnp.where(lane < 4, wy[b], 0.0)
        gathered = gathered + (tile if b == 0 else pltpu.roll(tile, 4 * b, 1))
    turned = jnp.concatenate([gathered, jnp.zeros((120, 128), F32)], axis=0).T[:SCEN]
    for shift in (8, 16, 32, 64):
        turned = turned + pltpu.roll(turned, shift, 1)
    group = lax.broadcasted_iota(jnp.int32, (SCEN, 128), 0)
    eighth = lax.broadcasted_iota(jnp.int32, (SCEN, 128), 1) // 8
    w_ref[0:1, :] = jnp.sum(jnp.where(group == eighth, turned, 0.0), axis=0, keepdims=True)
    w_ref[1:2, :] = jnp.sum(jnp.where(group == eighth + 16, turned, 0.0), axis=0, keepdims=True)

    drain(la.at[pl.ds(0, NY - 1)], la_s)
    drain(la.at[pl.ds(0, NY)], sb_s)
    drain(px.at[pl.ds(0, 4)], pt_s)
    drain(cost.at[0], ct_s)
    drain(yd.at[:, pl.ds(0, 6)], dd_s)
    drain(solt.at[:, pl.ds(0, SCEN * (NS - 1)), :], so_s)
    drain(mz.at[pl.ds(0, NZ - 1)], mz_s)
    drain(drt.at[:, :, pl.ds(0, SCEN * (NS - 1)), :], dr_s)
    drain(wy.at[pl.ds(0, NS - 1)], wy_s)


def body(
    tile_blocks, tile_row, tile_col, tile_count, column_costs, demand, primal_start, dual_start
):
    smem = pl.BlockSpec(memory_space=pltpu.SMEM)
    vmem = pl.BlockSpec(memory_space=pltpu.VMEM)
    dma = pltpu.SemaphoreType.DMA
    solution_, duals, residual, weight = pl.pallas_call(
        kernel,
        out_shape=(
            jax.ShapeDtypeStruct((512, 256), F32),
            jax.ShapeDtypeStruct((256, 256), F32),
            jax.ShapeDtypeStruct((256, 256), F32),
            jax.ShapeDtypeStruct((2, 128), F32),
        ),
        in_specs=[smem, smem, smem, vmem, vmem, vmem, vmem, vmem],
        out_specs=(vmem, vmem, vmem, vmem),
        scratch_shapes=[
            pltpu.VMEM((8, 256, 512), F32),
            pltpu.VMEM((1024, 1024), BF16),
            pltpu.VMEM((1024, 1024), BF16),
            pltpu.VMEM((2, 2, 256, 128), F32),
            pltpu.VMEM((2, 8, SCEN, 128), F32),
            pltpu.VMEM((4, 256, 128), F32),
            pltpu.VMEM((8, SCEN, 128), F32),
            pltpu.VMEM((2, 8, 128), F32),
            pltpu.VMEM((8, 128, 128), F32),
            pltpu.VMEM((8, 128), F32),
            pltpu.VMEM((8, 128), F32),
            pltpu.VMEM((2, 8, 128), F32),
            pltpu.VMEM((4, NX, 8, 128), F32),
            pltpu.VMEM((4, NZ, 8, 128), F32),
            pltpu.VMEM((HALVES, NZ, SR, 128), F32),
            pltpu.VMEM((HALVES, NZ - 1, SR, 128), F32),
            pltpu.VMEM((HALVES, NZ, SR, 128), F32),
            pltpu.VMEM((HALVES, W, 128), F32),
            pltpu.VMEM((2, HALVES, NX, 9, W, 128), F32),
            pltpu.VMEM((8, SCEN, 128), F32),
            pltpu.VMEM((2, 8, SCEN, 128), F32),
            pltpu.VMEM((4, 256, 128), F32),
            pltpu.VMEM((2, 2, 256, 128), F32),
            pltpu.VMEM((NZ, 8, 128), F32),
            pltpu.VMEM((NS, 8, 128), F32),
            dma, dma,
            dma, dma((NY,)),
            dma, dma((NY,)),
            dma, dma,
            dma, dma,
            dma((4,)), dma((4,)),
            dma((4,)), dma((4,)),
            dma((HALVES,)), dma((HALVES,)),
            dma((HALVES,)), dma((HALVES,)),
            dma((2, HALVES)), dma((2, HALVES)),
            dma, dma,
            dma, dma,
            dma, dma,
            dma, dma,
        ],
        compiler_params=pltpu.CompilerParams(
            collective_id=0, has_side_effects=True, vmem_limit_bytes=40 << 20
        ),
    )(
        tile_row, tile_col, tile_count, tile_blocks[0], column_costs.reshape(4, 128), demand, primal_start, dual_start
    )
    return solution_, duals, residual, weight.reshape(256)


def solution(mesh):
    return jax.shard_map(
        body,
        mesh=mesh,
        in_specs=(
            P("rows", "cols", None, None),
            P("rows", "cols"),
            P("rows", "cols"),
            P("rows", "cols"),
            P("cols"),
            P("rows", None),
            P("cols", None),
            P("rows", None),
        ),
        out_specs=(P("cols", None), P("rows", None), P("rows", None), P()),
        check_vma=False,
    )
```

time: 1920 us -> 168 us (0.09); the launches traced: 1890 us -> 168 us
  blocking collectives: 1150 us -> 0 us
  waiting for transfers between devices: 649 us -> 0 us
  Pallas kernels: 0 us -> 159 us
  matrix products: 37.3 us -> 0 us
  other arithmetic: 19.7 us -> 0 us
    psum x10 -> x0, blocking collectives: 682 us -> none  [the longest x4 465 us: body(): lax.psum(jnp.sum(jnp.square(new_dual - dual_now), axis=(0, 1)), 'rows')]
    psum x8 -> x0, waiting for transfers between devices: 649 us -> none  [the longest x4 375 us: body(): summed = lax.psum(partial_costs, 'rows')]
    pmax x6 -> x0, blocking collectives: 467 us -> none  [the longest x2 227 us: body(): col_max = lax.pmax(col_part, 'rows')]
    pallas_call x0 -> x1, Pallas kernels: none -> 159 us  [body(): pl.pallas_call(kernel, out_shape=(jax.ShapeDtypeStruct((512, 256), F32),...]
    dot_general x32 -> x0, matrix products: 37.3 us -> none  [the longest x4 8.3 us: backward(): return jnp.einsum('tc,tjs->cjs', col_hot, product, precision=HIGHEST)]
  transfers between devices with their start and end apart: 8 -> 0, of which waited for: 7 -> 0; matrix products, arithmetic and copies ran while one was open for 0% -> 0% of each run, Pallas kernels for 0% -> 0%
where the time goes in v1:
time: 168 us
  Pallas kernels  159 us (95%)
  local copies, waits for them, and re-layouts  7.32 us (4%)
    pallas_call x1, Pallas kernels, body(): pl.pallas_call(kernel, out_shape=(jax.ShapeDtypeStruct((512, 256), F32),...  159 us
    unnamed x18, local copies, waits for them, and re-layouts  7.32 us

profile of v1, /device:TPU:1, one launch (start us, length us, event | category | flops | bytes accessed | tf_op | source)
XLA Modules:
  0.0 167.7 jit_solution(17254610004185360272)
XLA Ops:
  1.3 0.0 copy-start.4
  1.3 0.0 copy-start.5
  1.3 0.0 copy-start.6
  1.3 0.7 copy-done.4
  2.0 0.0 copy-done.5
  2.0 0.0 copy-done.6
  2.0 0.0 copy-start
  2.0 1.0 copy-done
  3.0 0.0 copy-start.1
  3.0 0.9 copy-done.1
  4.0 0.0 copy-start.2
  4.0 0.9 copy-done.2
  4.9 0.0 copy-start.3
  4.9 0.9 copy-done.3
  5.9 159.1 %shard_map.111 = (f32[512,256]{1,0:T(8,128)S(1)}, f32[256,256]{1,0:T(8,128)S(1)}, f32[256,256]{1,0:T(8,128)S(1)}, f32[2,128]{1,0:T(2,128)S(1)}) custom-call(s32[1,8]{1,0:T(1,128)S(1)} %copy-done.5, s32[1,8]{1,0:T(1,128)S(1)} %copy-done.6, s32[1,1]{1,0:T(1,128)S(6)} %copy.16.count_ref, bf16[8,128,128]{2,1,0:T(8,128)(2,1)S(1)} %bitcast.3, ...), custom_call_target="tpu_custom_call" | custom-call | tf_op jit(solution)/shard_map/pallas_call | solution.py:384
  165.0 0.8 copy.17
  165.8 0.7 copy.18
  166.5 0.7 copy.19
  167.2 0.6 copy.20
Async XLA Ops:
  1.3 0.7 copy-start.4
  1.3 0.7 copy-start.5
  1.3 0.7 copy-start.6
  2.0 1.0 copy-start
  3.0 0.9 copy-start.1
  4.0 0.9 copy-start.2
  4.9 0.9 copy-start.3

commit v2 on v1

--- a/solution.py
+++ b/solution.py
@@ -9,6 +9,7 @@
 
 NZ, NY, NX, NK = 16, 4, 4, 2
 NS = NY * NK
+PLANE = NX * NY * NK
 SCEN = 32
 HALVES = 2
 W = SCEN // HALVES
@@ -20,10 +21,10 @@
 
 
 def kernel(
-    row_ref, col_ref, count_ref, tiles_ref, costs_ref, demand_ref, primal_ref, dual_ref,
-    sol_ref, dv_ref, res_ref, w_ref,
-    la, ab, at, dd, yd, pt, px, cost, rsc, rsr, csr, part, rx, cz, g, rsb, gs, mrow, fx, xs, ydo, solt, drt, mz, wy,
-    dd_s, dd_r, la_s, la_r, sb_s, sb_r, pt_s, pt_r, ct_s, ct_r, rx_s, rx_r, cz_s, cz_r,
+    row_ref, col_ref, count_ref, tiles_hbm, costs_hbm, demand_hbm, primal_hbm, dual_hbm,
+    sol_hbm, dv_hbm, res_hbm, w_ref,
+    tiles_ref, costs_ref, demand_ref, primal_ref, dual_ref, in_s, sol_ref, dv_ref, res_ref, out_s, la, ab, at, dd, yd, pt, px, cost, rsc, rsr, csr, part, rp, cy, cz4, rx, cz, g, rsb, gs, mrow, fx, xs, ydo, solt, drt, mz, wy,
+    dd_s, dd_r, la_s, la_r, sb_s, sb_r, pt_s, pt_r, ct_s, ct_r, rp_s, rp_r, cy_s, cy_r, c4_s, c4_r, rx_s, rx_r, cz_s, cz_r,
     rs_s, rs_r, ag_s, ag_r, fx_s, fx_r, so_s, so_r, dr_s, dr_r, mz_s, mz_r, wy_s, wy_r,
 ):
     rows, cols = lax.axis_index("rows"), lax.axis_index("cols")
@@ -58,17 +59,34 @@
     x_others = [(x + d) % NX for d in (2, 1, 3)]
     s_others = [(s + d) % NS for d in (4, 3, 5, 2, 6, 1, 7)]
 
+    me = y * NX * NK + cols
+
+    def plane(send):
+        def step(d, carry):
+            other = (me + d) % PLANE
+            send((z * NY + other // (NX * NK), other % (NX * NK)))
+            return carry
+
+        lax.fori_loop(1, PLANE, step, 0)
+
     barrier = pltpu.get_barrier_semaphore()
 
-    def greet(d, zz):
-        pl.semaphore_signal(barrier, inc=1, device_id=dev(zz, y, x, k), device_id_type=MESH)
-
-    z_far_first(greet)
-    for xx in x_others:
-        pl.semaphore_signal(barrier, inc=1, device_id=dev(z, y, xx, k), device_id_type=MESH)
-    for ss in s_others:
-        pl.semaphore_signal(barrier, inc=1, device_id=dev(z, ss // NK, x, ss % NK), device_id_type=MESH)
-
+    def greet(device):
+        pl.semaphore_signal(barrier, inc=1, device_id=device, device_id_type=MESH)
+
+    z_far_first(lambda d, zz: greet(dev(zz, y, x, k)))
+    plane(greet)
+    inputs = [
+        pltpu.make_async_copy(source, target, in_s.at[i])
+        for i, (source, target) in enumerate((
+            (tiles_hbm.at[0], tiles_ref), (dual_hbm, dual_ref), (demand_hbm, demand_ref),
+            (primal_hbm, primal_ref), (costs_hbm, costs_ref),
+        ))
+    ]
+    for copy in inputs:
+        copy.start()
+
+    inputs[0].wait()
     for rb in range(2):
         for cb in range(4):
             slot = jnp.int32(0)
@@ -78,12 +96,69 @@
             live = slot < count_ref[0, 0]
             block = tiles_ref[slot].astype(F32)
             la[s, 128 * rb : 128 * rb + 128, 128 * cb : 128 * cb + 128] = jnp.where(live, block, 0.0)
+    rsr[...] = jnp.ones((8, 128), F32)
+    csr[...] = jnp.ones((8, 128), F32)
+
+    def own_partials(scaled):
+        col_acc = [None] * 4
+        for a in range(2):
+            row_acc = None
+            if scaled:
+                row_scale = jnp.broadcast_to(rsr[pl.ds(2 * y + a, 1), :], (128, 128)).T
+            for c in range(4):
+                tile = jnp.abs(la[s, 128 * a : 128 * a + 128, 128 * c : 128 * c + 128])
+                if scaled:
+                    tile = tile * row_scale * csr[pl.ds(4 * k + c, 1), :]
+                row_acc = tile if c == 0 else jnp.maximum(row_acc, tile)
+                top = jnp.max(tile.reshape(16, 8, 128), axis=0)
+                col_acc[c] = top if a == 0 else jnp.maximum(col_acc[c], top)
+            part[0, a : a + 1, :] = jnp.max(row_acc.T, axis=0, keepdims=True)
+        for c in range(4):
+            part[1, c : c + 1, :] = jnp.max(col_acc[c], axis=0, keepdims=True)
+
+    def send_plane(use):
+        slot = cols * NY + y
+        rp[use, slot] = part[0, 0:2, :]
+        plane(lambda device: put(rp.at[use, slot], rp.at[use, slot], rp_s.at[use], rp_r.at[use], device))
+
+    def rescale_rows(use):
+        drain(rp.at[use, pl.ds(0, PLANE - 1)], rp_r.at[use])
+        for yy in range(NY):
+            top = rp[use, yy]
+            for cc in range(1, NX * NK):
+                top = jnp.maximum(top, rp[use, cc * NY + yy])
+            both = slice(2 * yy, 2 * yy + 2)
+            rsr[both, :] = rsr[both, :] / jnp.sqrt(top + EPSILON)
+        drain(rp.at[use, pl.ds(0, PLANE - 1)], rp_s.at[use])
+
+    def send_yk(use, value):
+        cy[use, s] = value
+        for ss in s_others:
+            put(cy.at[use, s], cy.at[use, s], cy_s.at[use], cy_r.at[use], dev(z, ss // NK, x, ss % NK))
+
+    def wait_yk(use):
+        drain(cy.at[use, pl.ds(0, NS - 1)], cy_r.at[use])
+        drain(cy.at[use, pl.ds(0, NS - 1)], cy_s.at[use])
+        tops = []
+        for kk in range(NK):
+            top = cy[use, kk]
+            for yy in range(1, NY):
+                top = jnp.maximum(top, cy[use, yy * NK + kk])
+            tops.append(top)
+        return jnp.concatenate(tops, axis=0)
+
+    own_partials(False)
+    inputs[1].wait()
+    inputs[2].wait()
     for a in range(2):
         dd[0, a] = dual_ref[128 * a : 128 * a + 128, :].T
         dd[1, a] = demand_ref[128 * a : 128 * a + 128, :].astype(F32).T
+    inputs[3].wait()
     for c in range(4):
         pt[c] = primal_ref[128 * c : 128 * c + 128, :].T
-    cost[k, 0:4, :] = costs_ref[...]
+    inputs[4].wait()
+    for c in range(4):
+        cost[k, c : c + 1, :] = costs_ref[128 * c : 128 * c + 128].reshape(1, 128)
     cost[k, 4:8, :] = jnp.zeros((4, 128), F32)
     for a in range(2):
         for kind in range(2):
@@ -91,7 +166,10 @@
     for c in range(4):
         px[4 * k + c] = pt[c, scen(s), :]
 
-    pl.semaphore_wait(barrier, NZ - 1 + NX - 1 + NS - 1)
+    pl.semaphore_wait(barrier, NZ - 1 + PLANE - 1)
+
+    send_yk(0, part[1, 0:4, :])
+    send_plane(0)
 
     put(la.at[s], la.at[s], sb_s, sb_r.at[y], sibling)
     put(
@@ -102,19 +180,22 @@
         put(
             dd.at[:, :, scen(yy * NK + k), :], yd.at[:, pl.ds(2 * y, 2)], dd_s, dd_r, dev(z, yy, x, k)
         )
-    for yy in y_others:
-        put(la.at[s], la.at[s], la_s, la_r.at[y], dev(z, yy, x, k))
-    for d in (3, 1, 2):
-        yy = (y + d) % NY
-        block = yy * NK + k
-        drain(la.at[block], la_r.at[yy])
-        put(la.at[block], la.at[block], sb_s, sb_r.at[yy], sibling)
-    for yy in range(NY):
-        drain(la.at[yy * NK + 1 - k], sb_r.at[yy])
-    drain(px.at[pl.ds(0, 4)], pt_r)
-    drain(cost.at[0], ct_r)
-    drain(yd.at[:, pl.ds(0, 6)], dd_r)
-
+    up, down = (y + 1) % NY, (y + 3) % NY
+
+    def half(yy, n):
+        return la.at[yy * NK + k, 128 * n : 128 * n + 128]
+
+    def pass_on(yy, n, to):
+        put(half(yy, n), half(yy, n), la_s, la_r.at[n, yy], dev(z, to, x, k))
+
+    def arrived(yy, n):
+        drain(half(yy, n), la_r.at[n, yy])
+        put(half(yy, n), half(yy, n), sb_s, sb_r.at[yy], sibling)
+
+    pass_on(y, 0, up)
+    pass_on(y, 1, down)
+    pass_on(y, 1, up)
+    pass_on(y, 0, down)
     def partials(op, reduce, scaled):
         def step(i, accs):
             row_acc, new = None, []
@@ -156,14 +237,6 @@
         drain(cz.at[use, pl.ds(0, NZ - 1)], cz_r.at[use])
         drain(cz.at[use, pl.ds(0, NZ - 1)], cz_s.at[use])
 
-    def rescale(use):
-        wait_x(use)
-        rsr[...] = rsr[...] / jnp.sqrt(jnp.max(rx[use], axis=0) + EPSILON)
-        for i in range(8):
-            rsc[i] = jnp.broadcast_to(rsr[i : i + 1, :], (128, 128)).T
-        wait_z(use)
-        csr[...] = csr[...] / jnp.sqrt(jnp.max(cz[use], axis=0) + EPSILON)
-
     def product(value, matrix):
         high = value.astype(BF16)
         low = (value - high.astype(F32)).astype(BF16)
@@ -198,47 +271,64 @@
     def part_of(h):
         return slice(h * W, (h + 1) * W)
 
-    rsr[...] = jnp.ones((8, 128), F32)
-    csr[...] = jnp.ones((8, 128), F32)
-    partials(jnp.maximum, jnp.max, False)
-    send_x(0, part[0])
-    send_z(0, part[1])
+    send_z(0, wait_yk(0))
+    rescale_rows(0)
+    arrived(down, 0)
+    pass_on(down, 0, up)
+    arrived(up, 1)
+    pass_on(up, 1, down)
+    wait_z(0)
+    csr[...] = csr[...] / jnp.sqrt(jnp.max(cz[0], axis=0) + EPSILON)
+    own_partials(True)
+    cz4[z] = part[1, 0:4, :]
+    z_far_first(lambda d, zz: put(cz4.at[z], cz4.at[z], c4_s, c4_r, dev(zz, y, x, k)))
+    send_plane(1)
+    arrived(up, 0)
+    arrived(down, 1)
+    arrived((y + 2) % NY, 0)
+    arrived((y + 2) % NY, 1)
+    rescale_rows(1)
+    drain(cz4.at[pl.ds(0, NZ - 1)], c4_r)
+    drain(cz4.at[pl.ds(0, NZ - 1)], c4_s)
+    send_yk(1, jnp.max(cz4[...], axis=0))
+    for yy in range(NY):
+        drain(la.at[yy * NK + 1 - k], sb_r.at[yy])
+    drain(yd.at[:, pl.ds(0, 6)], dd_r)
     for b in range(8):
         ab[256 * (b // 2) : 256 * (b // 2) + 256, 512 * (b % 2) : 512 * (b % 2) + 512] = la[b].astype(BF16)
+    for i in range(8):
+        rsc[i] = jnp.broadcast_to(rsr[i : i + 1, :], (128, 128)).T
     for h in range(HALVES):
         backward(h, [yd[0, i, part_of(h), :] for i in range(8)], jnp.zeros((W, 128), F32))
-    rescale(0)
-    partials(jnp.maximum, jnp.max, True)
-    send_x(1, part[0])
+    csr[...] = csr[...] / jnp.sqrt(wait_yk(1) + EPSILON)
+    partials(jnp.add, jnp.sum, True)
+    send_x(0, part[0])
     send_z(1, part[1])
+    wait_x(0)
+    send_z(2, rx[0, 0] + rx[0, 1] + rx[0, 2] + rx[0, 3])
     for h in range(HALVES):
         sum_and_spread(h)
     for b in range(8):
         at[512 * (b % 2) : 512 * (b % 2) + 512, 256 * (b // 2) : 256 * (b // 2) + 256] = la[b].T.astype(BF16)
-    rescale(1)
-    partials(jnp.add, jnp.sum, True)
-    send_x(2, part[0])
-    send_z(2, part[1])
+    wait_z(1)
+    col_sum = cz[1, 0]
+    for i in range(1, NZ):
+        col_sum = col_sum + cz[1, i]
+    send_x(1, col_sum)
+    drain(px.at[pl.ds(0, 4)], pt_r)
+    drain(cost.at[0], ct_r)
     for i in range(8):
         yd[0, i] = yd[0, i] / rsr[i : i + 1, :]
         yd[1, i] = yd[1, i] * rsr[i : i + 1, :]
         px[i] = px[i] / csr[i : i + 1, :]
     part[1] = csr[...] * jnp.concatenate([cost[0, 0:4, :], cost[1, 0:4, :]], axis=0)
-    wait_x(2)
-    row_sum = rx[2, 0] + rx[2, 1] + rx[2, 2] + rx[2, 3]
-    send_z(3, row_sum)
+    wait_x(1)
     wait_z(2)
-    col_sum = cz[2, 0]
-    for i in range(1, NZ):
-        col_sum = col_sum + cz[2, i]
-    send_x(3, col_sum)
-    wait_x(3)
-    wait_z(3)
 
     def largest(tiles):
         return jnp.max(jnp.max(jnp.max(tiles, axis=0), axis=1, keepdims=True), axis=0, keepdims=True)
 
-    step_size = 0.95 / jnp.sqrt(largest(cz[3]) * largest(rx[3]))
+    step_size = 0.95 / jnp.sqrt(largest(cz[2]) * largest(rx[1]))
 
     weight = [jnp.ones((W, 1), F32) for _ in range(HALVES)]
     primal_moves = [None] * HALVES
@@ -338,6 +428,12 @@
     drain(solt.at[:, pl.ds(0, SCEN * (NS - 1)), :], so_r)
     for c in range(4):
         sol_ref[128 * c : 128 * c + 128, :] = solt[c].T
+    outputs = [
+        pltpu.make_async_copy(sol_ref, sol_hbm, out_s.at[0]),
+        pltpu.make_async_copy(dv_ref, dv_hbm, out_s.at[1]),
+        pltpu.make_async_copy(res_ref, res_hbm, out_s.at[2]),
+    ]
+    outputs[0].start()
     drain(mz.at[pl.ds(0, NZ - 1)], mz_r)
     moved = mz[0]
     for i in range(1, NZ):
@@ -351,6 +447,8 @@
     for a in range(2):
         dv_ref[128 * a : 128 * a + 128, :] = drt[0, a].T
         res_ref[128 * a : 128 * a + 128, :] = drt[1, a].T
+    outputs[1].start()
+    outputs[2].start()
     drain(wy.at[pl.ds(0, NS - 1)], wy_r)
     gathered = jnp.zeros((8, 128), F32)
     for b in range(NS):
@@ -361,8 +459,10 @@
         turned = turned + pltpu.roll(turned, shift, 1)
     group = lax.broadcasted_iota(jnp.int32, (SCEN, 128), 0)
     eighth = lax.broadcasted_iota(jnp.int32, (SCEN, 128), 1) // 8
-    w_ref[0:1, :] = jnp.sum(jnp.where(group == eighth, turned, 0.0), axis=0, keepdims=True)
-    w_ref[1:2, :] = jnp.sum(jnp.where(group == eighth + 16, turned, 0.0), axis=0, keepdims=True)
+    w_ref[0:128] = jnp.sum(jnp.where(group == eighth, turned, 0.0), axis=0)
+    w_ref[128:256] = jnp.sum(jnp.where(group == eighth + 16, turned, 0.0), axis=0)
+    for copy in outputs:
+        copy.wait()
 
     drain(la.at[pl.ds(0, NY - 1)], la_s)
     drain(la.at[pl.ds(0, NY)], sb_s)
@@ -375,23 +475,47 @@
     drain(wy.at[pl.ds(0, NS - 1)], wy_s)
 
 
+def hand_over(*refs):
+    sources, targets, held, sems = refs[:4], refs[4:8], refs[8:12], refs[12]
+    first = [pltpu.make_async_copy(sources[i], held[i], sems.at[0, i]) for i in range(4)]
+    second = [pltpu.make_async_copy(held[i], targets[i], sems.at[1, i]) for i in range(4)]
+    for copy in first:
+        copy.start()
+    for i in (3, 1, 2, 0):
+        first[i].wait()
+        second[i].start()
+    for copy in second:
+        copy.wait()
+
+
 def body(
     tile_blocks, tile_row, tile_col, tile_count, column_costs, demand, primal_start, dual_start
 ):
     smem = pl.BlockSpec(memory_space=pltpu.SMEM)
     vmem = pl.BlockSpec(memory_space=pltpu.VMEM)
+    hbm = pl.BlockSpec(memory_space=pltpu.HBM)
     dma = pltpu.SemaphoreType.DMA
-    solution_, duals, residual, weight = pl.pallas_call(
+    results = pl.pallas_call(
         kernel,
         out_shape=(
             jax.ShapeDtypeStruct((512, 256), F32),
             jax.ShapeDtypeStruct((256, 256), F32),
             jax.ShapeDtypeStruct((256, 256), F32),
-            jax.ShapeDtypeStruct((2, 128), F32),
+            jax.ShapeDtypeStruct((SCEN * NS,), F32),
         ),
-        in_specs=[smem, smem, smem, vmem, vmem, vmem, vmem, vmem],
-        out_specs=(vmem, vmem, vmem, vmem),
+        in_specs=[smem, smem, smem, hbm, hbm, hbm, hbm, hbm],
+        out_specs=(hbm, hbm, hbm, vmem),
         scratch_shapes=[
+            pltpu.VMEM((8, 128, 128), BF16),
+            pltpu.VMEM((512,), F32),
+            pltpu.VMEM((256, 256), jnp.int32),
+            pltpu.VMEM((512, 256), F32),
+            pltpu.VMEM((256, 256), F32),
+            dma((5,)),
+            pltpu.VMEM((512, 256), F32),
+            pltpu.VMEM((256, 256), F32),
+            pltpu.VMEM((256, 256), F32),
+            dma((3,)),
             pltpu.VMEM((8, 256, 512), F32),
             pltpu.VMEM((1024, 1024), BF16),
             pltpu.VMEM((1024, 1024), BF16),
@@ -404,8 +528,11 @@
             pltpu.VMEM((8, 128), F32),
             pltpu.VMEM((8, 128), F32),
             pltpu.VMEM((2, 8, 128), F32),
-            pltpu.VMEM((4, NX, 8, 128), F32),
-            pltpu.VMEM((4, NZ, 8, 128), F32),
+            pltpu.VMEM((2, PLANE, 2, 128), F32),
+            pltpu.VMEM((2, NS, 4, 128), F32),
+            pltpu.VMEM((NZ, 4, 128), F32),
+            pltpu.VMEM((2, NX, 8, 128), F32),
+            pltpu.VMEM((3, NZ, 8, 128), F32),
             pltpu.VMEM((HALVES, NZ, SR, 128), F32),
             pltpu.VMEM((HALVES, NZ - 1, SR, 128), F32),
             pltpu.VMEM((HALVES, NZ, SR, 128), F32),
@@ -418,12 +545,15 @@
             pltpu.VMEM((NZ, 8, 128), F32),
             pltpu.VMEM((NS, 8, 128), F32),
             dma, dma,
+            dma, dma((2, NY)),
             dma, dma((NY,)),
-            dma, dma((NY,)),
-            dma, dma,
-            dma, dma,
-            dma((4,)), dma((4,)),
-            dma((4,)), dma((4,)),
+            dma, dma,
+            dma, dma,
+            dma((2,)), dma((2,)),
+            dma((2,)), dma((2,)),
+            dma, dma,
+            dma((2,)), dma((2,)),
+            dma((3,)), dma((3,)),
             dma((HALVES,)), dma((HALVES,)),
             dma((HALVES,)), dma((HALVES,)),
             dma((2, HALVES)), dma((2, HALVES)),
@@ -433,12 +563,19 @@
             dma, dma,
         ],
         compiler_params=pltpu.CompilerParams(
-            collective_id=0, has_side_effects=True, vmem_limit_bytes=40 << 20
+            collective_id=0, has_side_effects=True, vmem_limit_bytes=60 << 20
         ),
     )(
-        tile_row, tile_col, tile_count, tile_blocks[0], column_costs.reshape(4, 128), demand, primal_start, dual_start
+        tile_row, tile_col, tile_count, tile_blocks, column_costs, demand, primal_start, dual_start
     )
-    return solution_, duals, residual, weight.reshape(256)
+    return pl.pallas_call(
+        hand_over,
+        out_shape=tuple(jax.ShapeDtypeStruct(r.shape, F32) for r in results),
+        in_specs=[hbm] * 4,
+        out_specs=(hbm,) * 4,
+        scratch_shapes=[pltpu.VMEM(r.shape, F32) for r in results] + [dma((2, 4))],
+        compiler_params=pltpu.CompilerParams(vmem_limit_bytes=60 << 20),
+    )(*results)
 
 
 def solution(mesh):

time: 168 us -> 149 us (0.89)
  Pallas kernels: 159 us -> 148 us
  local copies, waits for them, and re-layouts: 7.32 us -> 0 us
    pallas_call x1, Pallas kernels: 159 us -> 146 us  [body(): pl.pallas_call(kernel, out_shape=(jax.ShapeDtypeStruct((512, 256), F32),...]
    unnamed x18 -> x0, local copies, waits for them, and re-layouts: 7.32 us -> none
    pallas_call x0 -> x1, Pallas kernels: none -> 2.15 us  [body(): pl.pallas_call(hand_over, out_shape=tuple((jax.ShapeDtypeStruct(r.shape,...]
where the time goes in v2:
time: 149 us
  Pallas kernels  148 us (99%)
    pallas_call x1, Pallas kernels, body(): pl.pallas_call(kernel, out_shape=(jax.ShapeDtypeStruct((512, 256), F32),...  146 us

profile of v2, /device:TPU:1, one launch (start us, length us, event | category | flops | bytes accessed | tf_op | source)
XLA Modules:
  0.0 149.0 jit_solution(16080308131576277394)
XLA Ops:
  1.3 145.6 %shard_map.111 = (f32[512,256]{1,0:T(8,128)}, f32[256,256]{1,0:T(8,128)}, f32[256,256]{1,0:T(8,128)}, f32[256]{0:T(256)}) custom-call(s32[1,8]{1,0:T(1,128)} %row_ref.1, s32[1,8]{1,0:T(1,128)} %col_ref.1, s32[1,1]{1,0:T(1,128)S(6)} %copy.12.count_ref, bf16[1,8,128,128]{3,2,1,0:T(8,128)(2,1)} %tiles_hbm.1, f32[512]{0:T(512)} %costs_hbm.1, ...), custom_call_target="tpu_custom_call" | custom-call | tf_op jit(solution)/shard_map/pallas_call | solution.py:498
  146.9 2.1 %shard_map.112 = (f32[512,256]{1,0:T(8,128)}, f32[256,256]{1,0:T(8,128)}, f32[256,256]{1,0:T(8,128)}, f32[256]{0:T(256)}) custom-call(f32[512,256]{1,0:T(8,128)} %get-tuple-element.8.refs_0_, f32[256,256]{1,0:T(8,128)} %get-tuple-element.9.refs_1_, f32[256,256]{1,0:T(8,128)} %get-tuple-element.10.refs_2_, f32[256]{0:T(256)} %get-tuple-element.11.refs_3_), custom_call_target="tpu_custom_call" | custom-call | tf_op jit(solution)/shard_map/pallas_call | solution.py:571

commit v3 on v2

--- a/solution.py
+++ b/solution.py
@@ -23,8 +23,8 @@
 def kernel(
     row_ref, col_ref, count_ref, tiles_hbm, costs_hbm, demand_hbm, primal_hbm, dual_hbm,
     sol_hbm, dv_hbm, res_hbm, w_ref,
-    tiles_ref, costs_ref, demand_ref, primal_ref, dual_ref, in_s, sol_ref, dv_ref, res_ref, out_s, la, ab, at, dd, yd, pt, px, cost, rsc, rsr, csr, part, rp, cy, cz4, rx, cz, g, rsb, gs, mrow, fx, xs, ydo, solt, drt, mz, wy,
-    dd_s, dd_r, la_s, la_r, sb_s, sb_r, pt_s, pt_r, ct_s, ct_r, rp_s, rp_r, cy_s, cy_r, c4_s, c4_r, rx_s, rx_r, cz_s, cz_r,
+    tiles_ref, costs_ref, demand_ref, primal_ref, dual_ref, in_s, sol_ref, dv_ref, res_ref, out_s, la, ab, at, dd, yd, pt, px, cost, rsr, csr, part, bp, bq, rp, cp, cy, cz4, cz, tz, g, rsb, gs, mrow, fx, xs, ydo, solt, drt, mz, wy,
+    dd_s, dd_r, la_s, la_r, sb_s, sb_r, pt_s, pt_r, ct_s, ct_r, bp_s, bp_r, rp_s, rp_r, cp_s, cp_r, cy_s, cy_r, c4_s, c4_r, cz_s, cz_r, tz_s, tz_r,
     rs_s, rs_r, ag_s, ag_r, fx_s, fx_r, so_s, so_r, dr_s, dr_r, mz_s, mz_r, wy_s, wy_r,
 ):
     rows, cols = lax.axis_index("rows"), lax.axis_index("cols")
@@ -99,7 +99,7 @@
     rsr[...] = jnp.ones((8, 128), F32)
     csr[...] = jnp.ones((8, 128), F32)
 
-    def own_partials(scaled):
+    def own_partials(op, reduce, scaled):
         col_acc = [None] * 4
         for a in range(2):
             row_acc = None
@@ -109,17 +109,28 @@
                 tile = jnp.abs(la[s, 128 * a : 128 * a + 128, 128 * c : 128 * c + 128])
                 if scaled:
                     tile = tile * row_scale * csr[pl.ds(4 * k + c, 1), :]
-                row_acc = tile if c == 0 else jnp.maximum(row_acc, tile)
-                top = jnp.max(tile.reshape(16, 8, 128), axis=0)
-                col_acc[c] = top if a == 0 else jnp.maximum(col_acc[c], top)
-            part[0, a : a + 1, :] = jnp.max(row_acc.T, axis=0, keepdims=True)
+                row_acc = tile if c == 0 else op(row_acc, tile)
+                top = reduce(tile.reshape(16, 8, 128), axis=0)
+                col_acc[c] = top if a == 0 else op(col_acc[c], top)
+            part[0, a : a + 1, :] = reduce(row_acc.T, axis=0, keepdims=True)
         for c in range(4):
-            part[1, c : c + 1, :] = jnp.max(col_acc[c], axis=0, keepdims=True)
+            part[1, c : c + 1, :] = reduce(col_acc[c], axis=0, keepdims=True)
+
+    slot_here = cols * NY + y
 
     def send_plane(use):
-        slot = cols * NY + y
-        rp[use, slot] = part[0, 0:2, :]
-        plane(lambda device: put(rp.at[use, slot], rp.at[use, slot], rp_s.at[use], rp_r.at[use], device))
+        rp[use, slot_here] = part[0, 0:2, :]
+        here = rp.at[use, slot_here]
+        plane(lambda device: put(here, here, rp_s.at[use], rp_r.at[use], device))
+
+    def send_cols(use):
+        cz4[use, z] = part[1, 0:4, :]
+        here = cz4.at[use, z]
+        z_far_first(lambda d, zz: put(here, here, c4_s.at[use], c4_r.at[use], dev(zz, y, x, k)))
+
+    def wait_cols(use):
+        drain(cz4.at[use, pl.ds(0, NZ - 1)], c4_r.at[use])
+        drain(cz4.at[use, pl.ds(0, NZ - 1)], c4_s.at[use])
 
     def rescale_rows(use):
         drain(rp.at[use, pl.ds(0, PLANE - 1)], rp_r.at[use])
@@ -147,7 +158,14 @@
             tops.append(top)
         return jnp.concatenate(tops, axis=0)
 
-    own_partials(False)
+    def product(value, matrix):
+        rows_ = value.shape[0]
+        high = value.astype(BF16)
+        low = (value - high.astype(F32)).astype(BF16)
+        both = jnp.dot(jnp.concatenate([high, low], axis=0), matrix, preferred_element_type=F32)
+        return both[:rows_] + both[rows_:]
+
+    own_partials(jnp.maximum, jnp.max, False)
     inputs[1].wait()
     inputs[2].wait()
     for a in range(2):
@@ -166,12 +184,19 @@
     for c in range(4):
         px[4 * k + c] = pt[c, scen(s), :]
 
+    first = product(jnp.concatenate([dd[0, 0], dd[0, 1]], axis=1), la[s].astype(BF16))
+    for b in range(NS):
+        for c in range(4):
+            bp[b, c] = first[SCEN * b : SCEN * b + SCEN, 128 * c : 128 * c + 128]
+    bq[s] = bp[s]
     pl.semaphore_wait(barrier, NZ - 1 + PLANE - 1)
 
     send_yk(0, part[1, 0:4, :])
     send_plane(0)
 
-    put(la.at[s], la.at[s], sb_s, sb_r.at[y], sibling)
+    for ss in s_others:
+        put(bp.at[ss], bq.at[s], bp_s, bp_r, dev(z, ss // NK, x, ss % NK))
+
     put(
         pt.at[:, scen(2 * y + 1 - k), :], px.at[pl.ds(4 * k, 4)], pt_s, pt_r, sibling
     )
@@ -180,6 +205,7 @@
         put(
             dd.at[:, :, scen(yy * NK + k), :], yd.at[:, pl.ds(2 * y, 2)], dd_s, dd_r, dev(z, yy, x, k)
         )
+    put(la.at[s], la.at[s], sb_s, sb_r.at[y], sibling)
     up, down = (y + 1) % NY, (y + 3) % NY
 
     def half(yy, n):
@@ -196,55 +222,18 @@
     pass_on(y, 1, down)
     pass_on(y, 1, up)
     pass_on(y, 0, down)
-    def partials(op, reduce, scaled):
-        def step(i, accs):
-            row_acc, new = None, []
-            for j in range(8):
-                tile = jnp.abs(
-                    la[
-                        2 * (i // 2) + j // 4,
-                        pl.ds(pl.multiple_of(128 * (i % 2), 128), 128),
-                        128 * (j % 4) : 128 * (j % 4) + 128,
-                    ]
-                )
-                if scaled:
-                    tile = tile * rsc[i] * csr[j : j + 1, :]
-                row_acc = tile if row_acc is None else op(row_acc, tile)
-                new.append(op(accs[j], reduce(tile.reshape(16, 8, 128), axis=0)))
-            part[0, pl.ds(i, 1), :] = reduce(row_acc.T, axis=0, keepdims=True)
-            return tuple(new)
-
-        accs = lax.fori_loop(0, 8, step, tuple(jnp.zeros((8, 128), F32) for _ in range(8)))
-        for j in range(8):
-            part[1, j : j + 1, :] = reduce(accs[j], axis=0, keepdims=True)
-
-    def send_x(use, value):
-        rx[use, x] = value
-        for xx in x_others:
-            put(rx.at[use, x], rx.at[use, x], rx_s.at[use], rx_r.at[use], dev(z, y, xx, k))
-
-    def send_z(use, value):
-        cz[use, z] = value
+    def send_z(value):
+        cz[z] = value
         z_far_first(
-            lambda d, zz: put(cz.at[use, z], cz.at[use, z], cz_s.at[use], cz_r.at[use], dev(zz, y, x, k))
+            lambda d, zz: put(cz.at[z], cz.at[z], cz_s, cz_r, dev(zz, y, x, k))
         )
 
-    def wait_x(use):
-        drain(rx.at[use, pl.ds(0, NX - 1)], rx_r.at[use])
-        drain(rx.at[use, pl.ds(0, NX - 1)], rx_s.at[use])
-
-    def wait_z(use):
-        drain(cz.at[use, pl.ds(0, NZ - 1)], cz_r.at[use])
-        drain(cz.at[use, pl.ds(0, NZ - 1)], cz_s.at[use])
-
-    def product(value, matrix):
-        high = value.astype(BF16)
-        low = (value - high.astype(F32)).astype(BF16)
-        both = jnp.dot(jnp.concatenate([high, low], axis=0), matrix[...], preferred_element_type=F32)
-        return both[:W] + both[W:]
+    def wait_z():
+        drain(cz.at[pl.ds(0, NZ - 1)], cz_r)
+        drain(cz.at[pl.ds(0, NZ - 1)], cz_s)
 
     def backward(h, duals, moves):
-        result = product(jnp.concatenate(duals, axis=1), ab)
+        result = product(jnp.concatenate(duals, axis=1), ab[...])
         for j in range(8):
             for q in range(2):
                 g[h, 2 * j + q, 0 : W // 2, :] = result[
@@ -253,6 +242,9 @@
         n = W // 16
         for i in range(16):
             g[h, i, W // 2 : SR, :] = moves[i * n : (i + 1) * n, :]
+        send_parts(h)
+
+    def send_parts(h):
         z_far_first(
             lambda d, zz: put(g.at[h, zz], rsb.at[h, d - 1], rs_s.at[h], rs_r.at[h], dev(zz, y, x, k))
         )
@@ -271,64 +263,91 @@
     def part_of(h):
         return slice(h * W, (h + 1) * W)
 
-    send_z(0, wait_yk(0))
+    send_z(wait_yk(0))
+    drain(bq.at[pl.ds(0, NS - 1)], bp_r)
+    for kk in range(NK):
+        total = bq[kk]
+        for yy in range(1, NY):
+            total = total + bq[yy * NK + kk]
+        for c in range(4):
+            for h in range(HALVES):
+                for q in range(2):
+                    top = h * W + q * (W // 2)
+                    g[h, 8 * kk + 2 * c + q, 0 : W // 2, :] = total[c, top : top + W // 2, :]
+    for h in range(HALVES):
+        for i in range(16):
+            g[h, i, W // 2 : SR, :] = jnp.zeros((W // 16, 128), F32)
+        send_parts(h)
     rescale_rows(0)
+    wait_z()
+    csr[...] = csr[...] / jnp.sqrt(jnp.max(cz[...], axis=0) + EPSILON)
+    own_partials(jnp.maximum, jnp.max, True)
+    send_cols(0)
+    send_plane(1)
     arrived(down, 0)
     pass_on(down, 0, up)
     arrived(up, 1)
     pass_on(up, 1, down)
-    wait_z(0)
-    csr[...] = csr[...] / jnp.sqrt(jnp.max(cz[0], axis=0) + EPSILON)
-    own_partials(True)
-    cz4[z] = part[1, 0:4, :]
-    z_far_first(lambda d, zz: put(cz4.at[z], cz4.at[z], c4_s, c4_r, dev(zz, y, x, k)))
-    send_plane(1)
+    for h in range(HALVES):
+        sum_and_spread(h)
+    rescale_rows(1)
+    wait_cols(0)
+    send_yk(1, jnp.max(cz4[0], axis=0))
+    csr[...] = csr[...] / jnp.sqrt(wait_yk(1) + EPSILON)
+    own_partials(jnp.add, jnp.sum, True)
+    send_cols(1)
+    send_plane(2)
+    drain(rp.at[2, pl.ds(0, PLANE - 1)], rp_r.at[2])
+    drain(rp.at[2, pl.ds(0, PLANE - 1)], rp_s.at[2])
+    tall = None
+    for yy in range(NY):
+        total = rp[2, yy]
+        for cc in range(1, NX * NK):
+            total = total + rp[2, cc * NY + yy]
+        tall = total if tall is None else jnp.maximum(tall, total)
+    tz[z, 0:1, :] = jnp.max(tall, axis=0, keepdims=True)
+    tallest = tz.at[z, 0:1]
+    z_far_first(lambda d, zz: put(tallest, tallest, tz_s, tz_r, dev(zz, y, x, k)))
+    wait_cols(1)
+    total = cz4[1, 0]
+    for i in range(1, NZ):
+        total = total + cz4[1, i]
+    cp[slot_here] = total
+    here = cp.at[slot_here]
+    plane(lambda device: put(here, here, cp_s, cp_r, device))
     arrived(up, 0)
     arrived(down, 1)
     arrived((y + 2) % NY, 0)
     arrived((y + 2) % NY, 1)
-    rescale_rows(1)
-    drain(cz4.at[pl.ds(0, NZ - 1)], c4_r)
-    drain(cz4.at[pl.ds(0, NZ - 1)], c4_s)
-    send_yk(1, jnp.max(cz4[...], axis=0))
     for yy in range(NY):
         drain(la.at[yy * NK + 1 - k], sb_r.at[yy])
-    drain(yd.at[:, pl.ds(0, 6)], dd_r)
     for b in range(8):
         ab[256 * (b // 2) : 256 * (b // 2) + 256, 512 * (b % 2) : 512 * (b % 2) + 512] = la[b].astype(BF16)
-    for i in range(8):
-        rsc[i] = jnp.broadcast_to(rsr[i : i + 1, :], (128, 128)).T
-    for h in range(HALVES):
-        backward(h, [yd[0, i, part_of(h), :] for i in range(8)], jnp.zeros((W, 128), F32))
-    csr[...] = csr[...] / jnp.sqrt(wait_yk(1) + EPSILON)
-    partials(jnp.add, jnp.sum, True)
-    send_x(0, part[0])
-    send_z(1, part[1])
-    wait_x(0)
-    send_z(2, rx[0, 0] + rx[0, 1] + rx[0, 2] + rx[0, 3])
-    for h in range(HALVES):
-        sum_and_spread(h)
     for b in range(8):
         at[512 * (b % 2) : 512 * (b % 2) + 512, 256 * (b // 2) : 256 * (b // 2) + 256] = la[b].T.astype(BF16)
-    wait_z(1)
-    col_sum = cz[1, 0]
-    for i in range(1, NZ):
-        col_sum = col_sum + cz[1, i]
-    send_x(1, col_sum)
     drain(px.at[pl.ds(0, 4)], pt_r)
     drain(cost.at[0], ct_r)
+    drain(yd.at[:, pl.ds(0, 6)], dd_r)
     for i in range(8):
         yd[0, i] = yd[0, i] / rsr[i : i + 1, :]
         yd[1, i] = yd[1, i] * rsr[i : i + 1, :]
         px[i] = px[i] / csr[i : i + 1, :]
     part[1] = csr[...] * jnp.concatenate([cost[0, 0:4, :], cost[1, 0:4, :]], axis=0)
-    wait_x(1)
-    wait_z(2)
-
-    def largest(tiles):
-        return jnp.max(jnp.max(jnp.max(tiles, axis=0), axis=1, keepdims=True), axis=0, keepdims=True)
-
-    step_size = 0.95 / jnp.sqrt(largest(cz[2]) * largest(rx[1]))
+    drain(cp.at[pl.ds(0, PLANE - 1)], cp_r)
+    drain(cp.at[pl.ds(0, PLANE - 1)], cp_s)
+    wide = None
+    for cc in range(NX * NK):
+        total = cp[cc * NY]
+        for yy in range(1, NY):
+            total = total + cp[cc * NY + yy]
+        wide = total if wide is None else jnp.maximum(wide, total)
+    drain(tz.at[pl.ds(0, NZ - 1), 0:1], tz_r)
+    drain(tz.at[pl.ds(0, NZ - 1), 0:1], tz_s)
+
+    def largest(tile):
+        return jnp.max(jnp.max(tile, axis=1, keepdims=True), axis=0, keepdims=True)
+
+    step_size = 0.95 / jnp.sqrt(largest(jnp.max(tz[:, 0:1, :], axis=0)) * largest(wide))
 
     weight = [jnp.ones((W, 1), F32) for _ in range(HALVES)]
     primal_moves = [None] * HALVES
@@ -363,7 +382,7 @@
                 px[j, part_of(h), :] = new
                 if last:
                     xs[j, part_of(h), :] = scale * new
-            image = product(jnp.concatenate(extended, axis=1), at)
+            image = product(jnp.concatenate(extended, axis=1), at[...])
             for i in range(8):
                 fx[slot, h, x, i] = image[:, 128 * i : 128 * i + 128]
             fx[slot, h, x, 8] = moves
@@ -406,17 +425,14 @@
                 backward(h, duals, moves)
             drain(fx.at[slot, h, pl.ds(0, NX - 1)], fx_s.at[slot, h])
 
-    lane = lax.broadcasted_iota(jnp.int32, (8, 128), 1)
-
-    def packed(columns):
-        column = jnp.concatenate(columns, axis=0)
-        tile = jnp.zeros((8, 128), F32)
-        for q in range(4):
-            tile = jnp.where(lane == q, column[8 * q : 8 * q + 8], tile)
-        return tile
-
-    mz[z] = packed(dual_moves)
-    z_far_first(lambda d, zz: put(mz.at[z], mz.at[z], mz_s, mz_r, dev(zz, y, x, k)))
+    def as_row(columns):
+        column = jnp.broadcast_to(jnp.concatenate(columns, axis=0), (SCEN, 128))
+        return jnp.concatenate([column, jnp.zeros((128 - SCEN, 128), F32)], axis=0).T[0:1]
+
+    mz[z, 0:1, :] = as_row(dual_moves)
+    mine = mz.at[z, 0:1]
+    z_far_first(lambda d, zz: put(mine, mine, mz_s, mz_r, dev(zz, y, x, k)))
+    old_weight, moved_primal = as_row(weight), as_row(primal_moves)
     for a in range(2):
         for kind in range(2):
             drt[kind, a, scen(s), :] = ydo[kind, 2 * y + a]
@@ -434,45 +450,40 @@
         pltpu.make_async_copy(res_ref, res_hbm, out_s.at[2]),
     ]
     outputs[0].start()
-    drain(mz.at[pl.ds(0, NZ - 1)], mz_r)
-    moved = mz[0]
+    drain(mz.at[pl.ds(0, NZ - 1), 0:1], mz_r)
+    moved = mz[0, 0:1, :]
     for i in range(1, NZ):
-        moved = moved + mz[i]
-    wy[s] = jnp.sqrt(
-        packed(weight) * jnp.sqrt((moved + EPSILON) / (packed(primal_moves) + EPSILON))
-    )
+        moved = moved + mz[i, 0:1, :]
+    wy[s, 0:1, :] = jnp.sqrt(old_weight * jnp.sqrt((moved + EPSILON) / (moved_primal + EPSILON)))
     for ss in s_others:
-        put(wy.at[s], wy.at[s], wy_s, wy_r, dev(z, ss // NK, x, ss % NK))
+        put(wy.at[s, 0:1], wy.at[s, 0:1], wy_s, wy_r, dev(z, ss // NK, x, ss % NK))
     drain(drt.at[:, :, pl.ds(0, SCEN * (NS - 1)), :], dr_r)
     for a in range(2):
         dv_ref[128 * a : 128 * a + 128, :] = drt[0, a].T
         res_ref[128 * a : 128 * a + 128, :] = drt[1, a].T
     outputs[1].start()
     outputs[2].start()
-    drain(wy.at[pl.ds(0, NS - 1)], wy_r)
-    gathered = jnp.zeros((8, 128), F32)
-    for b in range(NS):
-        tile = jnp.where(lane < 4, wy[b], 0.0)
-        gathered = gathered + (tile if b == 0 else pltpu.roll(tile, 4 * b, 1))
-    turned = jnp.concatenate([gathered, jnp.zeros((120, 128), F32)], axis=0).T[:SCEN]
-    for shift in (8, 16, 32, 64):
-        turned = turned + pltpu.roll(turned, shift, 1)
-    group = lax.broadcasted_iota(jnp.int32, (SCEN, 128), 0)
-    eighth = lax.broadcasted_iota(jnp.int32, (SCEN, 128), 1) // 8
-    w_ref[0:128] = jnp.sum(jnp.where(group == eighth, turned, 0.0), axis=0)
-    w_ref[128:256] = jnp.sum(jnp.where(group == eighth + 16, turned, 0.0), axis=0)
+    drain(wy.at[pl.ds(0, NS - 1), 0:1], wy_r)
+    every = jnp.concatenate([wy[b, 0:1, :] for b in range(NS)], axis=0)
+    low, high = every[0:1], every[4:5]
+    for b in range(1, 4):
+        moved_on = pltpu.roll(every, SCEN * b, 1)
+        low, high = low + moved_on[b : b + 1], high + moved_on[4 + b : 5 + b]
+    w_ref[0:128] = low.reshape(128)
+    w_ref[128:256] = high.reshape(128)
     for copy in outputs:
         copy.wait()
 
     drain(la.at[pl.ds(0, NY - 1)], la_s)
+    drain(bq.at[pl.ds(0, NS - 1)], bp_s)
     drain(la.at[pl.ds(0, NY)], sb_s)
     drain(px.at[pl.ds(0, 4)], pt_s)
     drain(cost.at[0], ct_s)
     drain(yd.at[:, pl.ds(0, 6)], dd_s)
     drain(solt.at[:, pl.ds(0, SCEN * (NS - 1)), :], so_s)
-    drain(mz.at[pl.ds(0, NZ - 1)], mz_s)
+    drain(mz.at[pl.ds(0, NZ - 1), 0:1], mz_s)
     drain(drt.at[:, :, pl.ds(0, SCEN * (NS - 1)), :], dr_s)
-    drain(wy.at[pl.ds(0, NS - 1)], wy_s)
+    drain(wy.at[pl.ds(0, NS - 1), 0:1], wy_s)
 
 
 def hand_over(*refs):
@@ -524,15 +535,17 @@
             pltpu.VMEM((4, 256, 128), F32),
             pltpu.VMEM((8, SCEN, 128), F32),
             pltpu.VMEM((2, 8, 128), F32),
-            pltpu.VMEM((8, 128, 128), F32),
             pltpu.VMEM((8, 128), F32),
             pltpu.VMEM((8, 128), F32),
             pltpu.VMEM((2, 8, 128), F32),
-            pltpu.VMEM((2, PLANE, 2, 128), F32),
+            pltpu.VMEM((NS, 4, SCEN, 128), F32),
+            pltpu.VMEM((NS, 4, SCEN, 128), F32),
+            pltpu.VMEM((3, PLANE, 2, 128), F32),
+            pltpu.VMEM((PLANE, 4, 128), F32),
             pltpu.VMEM((2, NS, 4, 128), F32),
-            pltpu.VMEM((NZ, 4, 128), F32),
-            pltpu.VMEM((2, NX, 8, 128), F32),
-            pltpu.VMEM((3, NZ, 8, 128), F32),
+            pltpu.VMEM((2, NZ, 4, 128), F32),
+            pltpu.VMEM((NZ, 8, 128), F32),
+            pltpu.VMEM((NZ, 8, 128), F32),
             pltpu.VMEM((HALVES, NZ, SR, 128), F32),
             pltpu.VMEM((HALVES, NZ - 1, SR, 128), F32),
             pltpu.VMEM((HALVES, NZ, SR, 128), F32),
@@ -549,11 +562,13 @@
             dma, dma((NY,)),
             dma, dma,
             dma, dma,
+            dma, dma,
+            dma((3,)), dma((3,)),
+            dma, dma,
             dma((2,)), dma((2,)),
             dma((2,)), dma((2,)),
             dma, dma,
-            dma((2,)), dma((2,)),
-            dma((3,)), dma((3,)),
+            dma, dma,
             dma((HALVES,)), dma((HALVES,)),
             dma((HALVES,)), dma((HALVES,)),
             dma((2, HALVES)), dma((2, HALVES)),

time: 149 us -> 147 us (0.987)
  Pallas kernels: 148 us -> 145 us
    pallas_call x1, Pallas kernels: 146 us -> 143 us  [body(): pl.pallas_call(kernel, out_shape=(jax.ShapeDtypeStruct((512, 256), F32),...]
where the time goes in v3:
time: 147 us; the launch traced here: 146 us
  Pallas kernels  145 us (99%)
    pallas_call x1, Pallas kernels, body(): pl.pallas_call(kernel, out_shape=(jax.ShapeDtypeStruct((512, 256), F32),...  143 us

profile of v3, /device:TPU:1, one launch (start us, length us, event | category | flops | bytes accessed | tf_op | source)
XLA Modules:
  0.0 146.3 jit_solution(11599673998662842426)
XLA Ops:
  1.3 142.9 %shard_map.111 = (f32[512,256]{1,0:T(8,128)}, f32[256,256]{1,0:T(8,128)}, f32[256,256]{1,0:T(8,128)}, f32[256]{0:T(256)}) custom-call(s32[1,8]{1,0:T(1,128)} %row_ref.1, s32[1,8]{1,0:T(1,128)} %col_ref.1, s32[1,1]{1,0:T(1,128)S(6)} %copy.12.count_ref, bf16[1,8,128,128]{3,2,1,0:T(8,128)(2,1)} %tiles_hbm.1, f32[512]{0:T(512)} %costs_hbm.1, ...), custom_call_target="tpu_custom_call" | custom-call | tf_op jit(solution)/shard_map/pallas_call | solution.py:509
  144.2 2.1 %shard_map.112 = (f32[512,256]{1,0:T(8,128)}, f32[256,256]{1,0:T(8,128)}, f32[256,256]{1,0:T(8,128)}, f32[256]{0:T(256)}) custom-call(f32[512,256]{1,0:T(8,128)} %get-tuple-element.8.refs_0_, f32[256,256]{1,0:T(8,128)} %get-tuple-element.9.refs_1_, f32[256,256]{1,0:T(8,128)} %get-tuple-element.10.refs_2_, f32[256]{0:T(256)} %get-tuple-element.11.refs_3_), custom_call_target="tpu_custom_call" | custom-call | tf_op jit(solution)/shard_map/pallas_call | solution.py:586

commit v4 on v3

--- a/solution.py
+++ b/solution.py
@@ -130,7 +130,6 @@
 
     def wait_cols(use):
         drain(cz4.at[use, pl.ds(0, NZ - 1)], c4_r.at[use])
-        drain(cz4.at[use, pl.ds(0, NZ - 1)], c4_s.at[use])
 
     def rescale_rows(use):
         drain(rp.at[use, pl.ds(0, PLANE - 1)], rp_r.at[use])
@@ -140,7 +139,6 @@
                 top = jnp.maximum(top, rp[use, cc * NY + yy])
             both = slice(2 * yy, 2 * yy + 2)
             rsr[both, :] = rsr[both, :] / jnp.sqrt(top + EPSILON)
-        drain(rp.at[use, pl.ds(0, PLANE - 1)], rp_s.at[use])
 
     def send_yk(use, value):
         cy[use, s] = value
@@ -149,7 +147,6 @@
 
     def wait_yk(use):
         drain(cy.at[use, pl.ds(0, NS - 1)], cy_r.at[use])
-        drain(cy.at[use, pl.ds(0, NS - 1)], cy_s.at[use])
         tops = []
         for kk in range(NK):
             top = cy[use, kk]
@@ -230,7 +227,6 @@
 
     def wait_z():
         drain(cz.at[pl.ds(0, NZ - 1)], cz_r)
-        drain(cz.at[pl.ds(0, NZ - 1)], cz_s)
 
     def backward(h, duals, moves):
         result = product(jnp.concatenate(duals, axis=1), ab[...])
@@ -258,12 +254,13 @@
         z_far_first(
             lambda d, zz: put(gs.at[h, z], gs.at[h, z], ag_s.at[h], ag_r.at[h], dev(zz, y, x, k))
         )
-        drain(rsb.at[h], rs_s.at[h])
 
     def part_of(h):
         return slice(h * W, (h + 1) * W)
 
     send_z(wait_yk(0))
+    rescale_rows(0)
+    wait_z()
     drain(bq.at[pl.ds(0, NS - 1)], bp_r)
     for kk in range(NK):
         total = bq[kk]
@@ -278,8 +275,6 @@
         for i in range(16):
             g[h, i, W // 2 : SR, :] = jnp.zeros((W // 16, 128), F32)
         send_parts(h)
-    rescale_rows(0)
-    wait_z()
     csr[...] = csr[...] / jnp.sqrt(jnp.max(cz[...], axis=0) + EPSILON)
     own_partials(jnp.maximum, jnp.max, True)
     send_cols(0)
@@ -298,7 +293,6 @@
     send_cols(1)
     send_plane(2)
     drain(rp.at[2, pl.ds(0, PLANE - 1)], rp_r.at[2])
-    drain(rp.at[2, pl.ds(0, PLANE - 1)], rp_s.at[2])
     tall = None
     for yy in range(NY):
         total = rp[2, yy]
@@ -334,7 +328,6 @@
         px[i] = px[i] / csr[i : i + 1, :]
     part[1] = csr[...] * jnp.concatenate([cost[0, 0:4, :], cost[1, 0:4, :]], axis=0)
     drain(cp.at[pl.ds(0, PLANE - 1)], cp_r)
-    drain(cp.at[pl.ds(0, PLANE - 1)], cp_s)
     wide = None
     for cc in range(NX * NK):
         total = cp[cc * NY]
@@ -342,7 +335,6 @@
             total = total + cp[cc * NY + yy]
         wide = total if wide is None else jnp.maximum(wide, total)
     drain(tz.at[pl.ds(0, NZ - 1), 0:1], tz_r)
-    drain(tz.at[pl.ds(0, NZ - 1), 0:1], tz_s)
 
     def largest(tile):
         return jnp.max(jnp.max(tile, axis=1, keepdims=True), axis=0, keepdims=True)
@@ -390,6 +382,7 @@
                 put(
                     fx.at[slot, h, x], fx.at[slot, h, x], fx_s.at[slot, h], fx_r.at[slot, h], dev(z, y, xx, k)
                 )
+            drain(rsb.at[h], rs_s.at[h])
             drain(gs.at[h, pl.ds(0, NZ - 1)], ag_s.at[h])
         if last:
             for c in range(4):
@@ -474,6 +467,14 @@
     for copy in outputs:
         copy.wait()
 
+    for use in range(3):
+        drain(rp.at[use, pl.ds(0, PLANE - 1)], rp_s.at[use])
+    for use in range(2):
+        drain(cy.at[use, pl.ds(0, NS - 1)], cy_s.at[use])
+        drain(cz4.at[use, pl.ds(0, NZ - 1)], c4_s.at[use])
+    drain(cz.at[pl.ds(0, NZ - 1)], cz_s)
+    drain(tz.at[pl.ds(0, NZ - 1), 0:1], tz_s)
+    drain(cp.at[pl.ds(0, PLANE - 1)], cp_s)
     drain(la.at[pl.ds(0, NY - 1)], la_s)
     drain(bq.at[pl.ds(0, NS - 1)], bp_s)
     drain(la.at[pl.ds(0, NY)], sb_s)

time: 147 us -> 146 us (level)
  no operation moved by 1% of the time
where the time goes in v4:
time: 146 us
  Pallas kernels  145 us (99%)
    pallas_call x1, Pallas kernels, body(): pl.pallas_call(kernel, out_shape=(jax.ShapeDtypeStruct((512, 256), F32),...  143 us

profile of v4, /device:TPU:1, one launch (start us, length us, event | category | flops | bytes accessed | tf_op | source)
XLA Modules:
  0.0 146.2 jit_solution(16862474820610750140)
XLA Ops:
  1.3 142.8 %shard_map.111 = (f32[512,256]{1,0:T(8,128)}, f32[256,256]{1,0:T(8,128)}, f32[256,256]{1,0:T(8,128)}, f32[256]{0:T(256)}) custom-call(s32[1,8]{1,0:T(1,128)} %row_ref.1, s32[1,8]{1,0:T(1,128)} %col_ref.1, s32[1,1]{1,0:T(1,128)S(6)} %copy.12.count_ref, bf16[1,8,128,128]{3,2,1,0:T(8,128)(2,1)} %tiles_hbm.1, f32[512]{0:T(512)} %costs_hbm.1, ...), custom_call_target="tpu_custom_call" | custom-call | tf_op jit(solution)/shard_map/pallas_call | solution.py:510
  144.1 2.1 %shard_map.112 = (f32[512,256]{1,0:T(8,128)}, f32[256,256]{1,0:T(8,128)}, f32[256,256]{1,0:T(8,128)}, f32[256]{0:T(256)}) custom-call(f32[512,256]{1,0:T(8,128)} %get-tuple-element.8.refs_0_, f32[256,256]{1,0:T(8,128)} %get-tuple-element.9.refs_1_, f32[256,256]{1,0:T(8,128)} %get-tuple-element.10.refs_2_, f32[256]{0:T(256)} %get-tuple-element.11.refs_3_), custom_call_target="tpu_custom_call" | custom-call | tf_op jit(solution)/shard_map/pallas_call | solution.py:587
